TPU v7x, 512 devices: a whole 4x4x16 slice. The times are simulated.
512 devices in a mesh: dp: 16 (over y, x), expert: 32 (over z, core).
Axes of the slice: x: 4, y: 4, z: 16, core: 2. Of those that a mesh axis runs over, the one named last changes fastest.
Arguments:
- tokens: bfloat16 [65536, 2560], P(('dp', 'expert')), may hold values from -6 to 6
- out_grad: bfloat16 [65536, 2560], P(('dp', 'expert')), may hold values from -0.59765625 to 0.59765625
- expert_ids: int32 [65536, 2], P(('dp', 'expert')), may hold values from 0 to 31, all different within a row; in each aligned block of 128 rows (0 to 127, 128 to 255, ...) at most 9 rows name the same one
- gate_values: float32 [65536, 2], P(('dp', 'expert')), may hold values from 0.05 to 0.5
- frozen_gate: bfloat16 [32, 2560, 768], P('expert', 'dp'), may hold values from -0.125 to 0.125
- frozen_up: bfloat16 [32, 2560, 768], P('expert', 'dp'), may hold values from -0.125 to 0.125
- locked_down_weight: bfloat16 [32, 2560, 768], P('expert', 'dp'), may hold values from -0.21875 to 0.21875
- gate_adapter_first: bfloat16 [32, 2560, 16], P('expert'), may hold values from -0.125 to 0.125
- gate_adapter_second: bfloat16 [32, 16, 768], P('expert'), may hold values from -1.5 to 1.5
- up_adapter_first: bfloat16 [32, 2560, 16], P('expert'), may hold values from -0.125 to 0.125
- up_adapter_second: bfloat16 [32, 16, 768], P('expert'), may hold values from -1.5 to 1.5
- down_adapter_first: bfloat16 [32, 768, 16], P('expert'), may hold values from -0.21875 to 0.21875
- down_adapter_second: bfloat16 [32, 16, 2560], P('expert'), may hold values from -1.5 to 1.5
Outputs:
- token_grad: bfloat16 [65536, 2560], P(('dp', 'expert'))
- gate_grad: float32 [65536, 2], P(('dp', 'expert'))
- grad_gate_in: float32 [32, 2560, 16], P('expert')
- grad_gate_out: float32 [32, 16, 768], P('expert')
- grad_up_in: float32 [32, 2560, 16], P('expert')
- grad_up_out: float32 [32, 16, 768], P('expert')
- grad_down_in: float32 [32, 768, 16], P('expert')
- grad_down_out: float32 [32, 16, 2560], P('expert')
Inputs may be any that keep to these rules, and one draw needn't show every extreme that they name: `expert_ids`: each token names 2 different experts. In the rows of one device no expert is named by more than 9 rows, a bound that some block reaches of one device.
All inputs are finite; a program needn't handle non-finite values.
Results may differ from a plain program's by a relative error of at most 0.025.
Values may be sent and summed in bfloat16 or wider, within the bound.
A program may use at most 128 MiB of HBM per device.

v0:
```python
import jax
import jax.numpy as jnp
from jax import lax
from jax.sharding import PartitionSpec as P

adapter_scale = 2.0


def matrix_product(left, right):
    return jnp.dot(left, right, preferred_element_type=jnp.float32)


def right_operand_flipped(left, right):
    return lax.dot_general(
        left, right, (((1,), (1,)), ((), ())), preferred_element_type=jnp.float32
    )


def left_operand_flipped(left, right):
    return lax.dot_general(
        left, right, (((0,), (0,)), ((), ())), preferred_element_type=jnp.float32
    )


def expert_adapter_rows(
    row_inputs,
    row_gradient,
    row_weighting,
    locked_gate_weight,
    locked_up_weight,
    gate_weight_matrix,
    up_weight_matrix,
    down_weight_matrix,
    gate_first_factor,
    gate_second_factor,
    up_first_factor,
    up_second_factor,
    down_first_factor,
    down_second_factor,
):
    gate_reduced_rows = matrix_product(row_inputs, gate_first_factor).astype(jnp.bfloat16)
    up_reduced_rows = matrix_product(row_inputs, up_first_factor).astype(jnp.bfloat16)
    gate_before_activation = locked_gate_weight + adapter_scale * matrix_product(
        gate_reduced_rows, gate_second_factor
    )
    up_before_activation = locked_up_weight + adapter_scale * matrix_product(
        up_reduced_rows, up_second_factor
    )
    sigmoid_gate = jax.nn.sigmoid(gate_before_activation)
    activation = gate_before_activation * sigmoid_gate
    hidden_rows = (activation * up_before_activation).astype(jnp.bfloat16)
    hidden_reduced_rows = matrix_product(hidden_rows, down_first_factor).astype(jnp.bfloat16)
    expert_result = right_operand_flipped(
        hidden_rows, down_weight_matrix
    ) + adapter_scale * matrix_product(hidden_reduced_rows, down_second_factor)
    grad_wide = row_gradient.astype(jnp.float32)
    slot_gate_values = jnp.sum(expert_result * grad_wide, axis=1)
    incoming_gradient = (row_weighting[:, None] * grad_wide).astype(jnp.bfloat16)
    incoming_reduced_gradient = right_operand_flipped(incoming_gradient, down_second_factor).astype(
        jnp.bfloat16
    )
    hidden_gradient = matrix_product(
        incoming_gradient, down_weight_matrix
    ) + adapter_scale * right_operand_flipped(incoming_reduced_gradient, down_first_factor)
    gate_gradient_before = (
        hidden_gradient
        * up_before_activation
        * sigmoid_gate
        * (1.0 + gate_before_activation * (1.0 - sigmoid_gate))
    ).astype(jnp.bfloat16)
    up_gradient_before = (hidden_gradient * activation).astype(jnp.bfloat16)
    gate_reduced_gradient = right_operand_flipped(gate_gradient_before, gate_second_factor).astype(
        jnp.bfloat16
    )
    up_reduced_gradient = right_operand_flipped(up_gradient_before, up_second_factor).astype(
        jnp.bfloat16
    )
    slot_gradient = right_operand_flipped(
        gate_gradient_before, gate_weight_matrix
    ) + right_operand_flipped(up_gradient_before, up_weight_matrix)
    slot_gradient = slot_gradient + adapter_scale * (
        right_operand_flipped(gate_reduced_gradient, gate_first_factor)
        + right_operand_flipped(up_reduced_gradient, up_first_factor)
    )
    slot_gradient = slot_gradient.astype(jnp.bfloat16)
    gradient_tuple = (
        adapter_scale * left_operand_flipped(row_inputs, gate_reduced_gradient),
        adapter_scale * left_operand_flipped(gate_reduced_rows, gate_gradient_before),
        adapter_scale * left_operand_flipped(row_inputs, up_reduced_gradient),
        adapter_scale * left_operand_flipped(up_reduced_rows, up_gradient_before),
        adapter_scale * left_operand_flipped(hidden_rows, incoming_reduced_gradient),
        adapter_scale * left_operand_flipped(hidden_reduced_rows, incoming_gradient),
    )
    return (slot_gradient, slot_gate_values, gradient_tuple)


def to_local(received, n_expert, local_count, capacity):
    tail = received.shape[1:]
    shaped = received.reshape((n_expert, local_count, capacity) + tail)
    return jnp.swapaxes(shaped, 0, 1).reshape((local_count, n_expert * capacity) + tail)


def from_local(stacked, n_expert, local_count, capacity):
    tail = stacked.shape[2:]
    shaped = stacked.reshape((local_count, n_expert, capacity) + tail)
    return jnp.swapaxes(shaped, 0, 1).reshape((n_expert * local_count * capacity,) + tail)


def per_device(
    tokens,
    out_grad,
    expert_ids,
    gate_values,
    frozen_gate,
    frozen_up,
    locked_down_weight,
    gate_adapter_first,
    gate_adapter_second,
    up_adapter_first,
    up_adapter_second,
    down_adapter_first,
    down_adapter_second,
):
    n_expert = lax.axis_size("expert")
    local_count = frozen_gate.shape[0]
    expert_total = local_count * n_expert
    token_count = tokens.shape[0]
    model_width = tokens.shape[1]
    fanout = expert_ids.shape[1]
    capacity = token_count * fanout * 9 // (8 * expert_total)
    flat_ids = expert_ids.reshape(-1)
    onehot = (flat_ids[:, None] == jnp.arange(expert_total, dtype=jnp.int32)[None, :]).astype(
        jnp.int32
    )
    before = jnp.cumsum(onehot, axis=0) - onehot
    slot_index = jnp.sum(before * onehot, axis=1)
    destination = flat_ids * capacity + slot_index
    owners = jnp.arange(token_count * fanout, dtype=jnp.int32) // fanout
    source = (
        jnp.full((expert_total * capacity,), token_count, jnp.int32).at[destination].set(owners)
    )
    weight_send = (
        jnp.zeros((expert_total * capacity,), jnp.float32)
        .at[destination]
        .set(gate_values.reshape(-1))
    )
    blank = jnp.zeros((1, model_width), jnp.bfloat16)
    input_send = jnp.concatenate([tokens, blank], axis=0)[source]
    grad_send = jnp.concatenate([out_grad, blank], axis=0)[source]
    input_recv, grad_recv, weight_recv = (
        lax.all_to_all(input_send, "expert", split_axis=0, concat_axis=0, tiled=True),
        lax.all_to_all(grad_send, "expert", split_axis=0, concat_axis=0, tiled=True),
        lax.all_to_all(
            weight_send.astype(jnp.bfloat16), "expert", split_axis=0, concat_axis=0, tiled=True
        ).astype(weight_send.dtype),
    )
    local_in = to_local(input_recv, n_expert, local_count, capacity)
    local_grad = to_local(grad_recv, n_expert, local_count, capacity)
    local_weight = to_local(weight_recv, n_expert, local_count, capacity)
    whole_gate, whole_up, whole_down = (
        lax.all_gather(frozen_gate, "dp", axis=1, tiled=True),
        lax.all_gather(frozen_up, "dp", axis=1, tiled=True),
        lax.all_gather(locked_down_weight, "dp", axis=1, tiled=True),
    )
    locked_gate_weight = jnp.einsum(
        "erd,edf->erf", local_in, whole_gate, preferred_element_type=jnp.float32
    )
    locked_up_weight = jnp.einsum(
        "erd,edf->erf", local_in, whole_up, preferred_element_type=jnp.float32
    )
    adapter_lists = [[], [], [], [], [], []]
    slot_gradient, slot_gate_values, gradient_tuple = expert_adapter_rows(
        local_in[0],
        local_grad[0],
        local_weight[0],
        locked_gate_weight[0],
        locked_up_weight[0],
        whole_gate[0],
        whole_up[0],
        whole_down[0],
        gate_adapter_first[0],
        gate_adapter_second[0],
        up_adapter_first[0],
        up_adapter_second[0],
        down_adapter_first[0],
        down_adapter_second[0],
    )
    grad_list = [slot_gradient]
    gate_list = [slot_gate_values]
    for which in range(6):
        adapter_lists[which].append(gradient_tuple[which])
    adapter_parts = [jnp.stack(parts, axis=0) for parts in adapter_lists]
    summed = (
        lax.psum(adapter_parts[0].astype(jnp.bfloat16), "dp").astype(jnp.float32),
        lax.psum(adapter_parts[1].astype(jnp.bfloat16), "dp").astype(jnp.float32),
        lax.psum(adapter_parts[2].astype(jnp.bfloat16), "dp").astype(jnp.float32),
        lax.psum(adapter_parts[3].astype(jnp.bfloat16), "dp").astype(jnp.float32),
        lax.psum(adapter_parts[4].astype(jnp.bfloat16), "dp").astype(jnp.float32),
        lax.psum(adapter_parts[5].astype(jnp.bfloat16), "dp").astype(jnp.float32),
    )
    grad_gate_in, grad_gate_out, grad_up_in, grad_up_out, grad_down_in, grad_down_out = summed
    grad_back = from_local(jnp.stack(grad_list, axis=0), n_expert, local_count, capacity)
    gate_back = from_local(jnp.stack(gate_list, axis=0), n_expert, local_count, capacity)
    grad_home, gate_home = (
        lax.all_to_all(grad_back, "expert", split_axis=0, concat_axis=0, tiled=True),
        lax.all_to_all(
            gate_back.astype(jnp.bfloat16), "expert", split_axis=0, concat_axis=0, tiled=True
        ).astype(gate_back.dtype),
    )
    picked = grad_home[destination].astype(jnp.float32).reshape(token_count, fanout, model_width)
    token_grad = jnp.sum(picked, axis=1).astype(jnp.bfloat16)
    gate_grad = gate_home[destination].reshape(token_count, fanout)
    return (
        token_grad,
        gate_grad,
        grad_gate_in,
        grad_gate_out,
        grad_up_in,
        grad_up_out,
        grad_down_in,
        grad_down_out,
    )


def solution(mesh):
    return jax.shard_map(
        per_device,
        mesh=mesh,
        in_specs=(
            P(("dp", "expert"), None),
            P(("dp", "expert"), None),
            P(("dp", "expert"), None),
            P(("dp", "expert"), None),
            P("expert", "dp", None),
            P("expert", "dp", None),
            P("expert", "dp", None),
            P("expert", None, None),
            P("expert", None, None),
            P("expert", None, None),
            P("expert", None, None),
            P("expert", None, None),
            P("expert", None, None),
        ),
        out_specs=(
            P(("dp", "expert"), None),
            P(("dp", "expert"), None),
            P("expert", None, None),
            P("expert", None, None),
            P("expert", None, None),
            P("expert", None, None),
            P("expert", None, None),
            P("expert", None, None),
        ),
        check_vma=False,
    )
```

profile of v0, /device:TPU:1, one launch (start us, length us, event | category | flops | bytes accessed | tf_op | source)
XLA Modules:
  0.0 604.5 jit_solution(16233805601828445518)
XLA Ops:
  12.6 1.4 scatter_custom_fusion
  14.7 16.7 %all-to-all-start = ((bf16[32,9,1]{1,2,0:T(2,128)(2,1)}), bf16[32,9,1]{1,2,0:T(2,128)(2,1)S(1)}, u32[]{:S(2)}, u32[]{:S(2)}) async-start(bf16[32,9,1]{1,2,0:T(2,128)(2,1)} %all_to_all.40), calls=%async_computation | async-start | bytes 32768 | tf_op jit(solution)/shard_map/all_to_all | solution.py:153
  31.5 1.4 scatter_custom_fusion.1
  32.9 1.2 concatenate.6
  34.1 2.6 gather_fusion
  36.7 1.9 all_to_all.32
  38.6 4.6 all-to-all-done
  43.2 7.5 %all-to-all-start.1 = ((bf16[32,9,2560]{2,1,0:T(8,128)(2,1)}), bf16[32,9,2560]{2,1,0:T(8,128)(2,1)S(1)}, u32[]{:S(2)}, u32[]{:S(2)}) async-start(bf16[32,9,2560]{2,1,0:T(8,128)(2,1)} %all_to_all.32), calls=%async_computation.1 | async-start | bytes 5242880 | tf_op jit(solution)/shard_map/all_to_all | solution.py:152
  50.7 1.1 concatenate.7
  51.9 3.1 gather_fusion.1
  55.0 2.9 all_to_all.34
  57.8 112.5 %all-to-all-done.1 = bf16[32,9,2560]{2,1,0:T(8,128)(2,1)S(1)} async-done(((bf16[32,9,2560]{2,1,0:T(8,128)(2,1)}), bf16[32,9,2560]{2,1,0:T(8,128)(2,1)S(1)}, u32[]{:S(2)}, u32[]{:S(2)}) %all-to-all-start.1) | async-done | bytes 1474592 | tf_op jit(solution)/shard_map/all_to_all | solution.py:152
  170.3 6.7 %all-to-all-start.2 = ((bf16[32,9,2560]{2,1,0:T(8,128)(2,1)}), bf16[32,9,2560]{2,1,0:T(8,128)(2,1)}, u32[]{:S(2)}, u32[]{:S(2)}) async-start(bf16[32,9,2560]{2,1,0:T(8,128)(2,1)} %all_to_all.34), calls=%async_computation.2 | async-start | bytes 5242880 | tf_op jit(solution)/shard_map/all_to_all | solution.py:151
  177.7 2.0 multiply_convert_fusion
  179.8 2.9 convert_element_type.158
  182.7 1.9 reshape.147
  184.6 112.0 %all-to-all-done.2 = bf16[32,9,2560]{2,1,0:T(8,128)(2,1)} async-done(((bf16[32,9,2560]{2,1,0:T(8,128)(2,1)}), bf16[32,9,2560]{2,1,0:T(8,128)(2,1)}, u32[]{:S(2)}, u32[]{:S(2)}) %all-to-all-start.2) | async-done | bytes 1474592 | tf_op jit(solution)/shard_map/all_to_all | solution.py:151
  296.6 2.0 reshape.142
  299.2 1.2 convolution_convert_fusion.1
  300.8 3.4 fusion.7
  304.3 1.3 fusion.24
  305.6 3.4 fusion.14
  309.0 1.3 fusion.26
  310.3 3.5 fusion.10
  314.8 2.2 fusion.34
  317.0 0.9 convolution_convert_fusion.4
  318.1 1.3 fusion.12
  321.4 6.7 %all-to-all-start.4 = ((bf16[32,9,1]{1,2,0:T(2,128)(2,1)}), bf16[32,9,1]{1,2,0:T(2,128)(2,1)}, u32[]{:S(2)}, u32[]{:S(2)}) async-start(bf16[32,9,1]{1,2,0:T(2,128)(2,1)} %convert_element_type.200), calls=%async_computation.4 | async-start | bytes 32768 | tf_op jit(solution)/shard_map/all_to_all | solution.py:206
  328.1 3.6 fusion.5
  331.8 1.3 convolution_add_fusion.1
  334.2 1.9 all_to_all.36
  336.1 3.7 all-to-all-done.4
  339.8 8.7 %all-to-all-start.3 = ((bf16[32,9,2560]{2,1,0:T(8,128)(2,1)}), bf16[32,9,2560]{2,1,0:T(8,128)(2,1)}, u32[]{:S(2)}, u32[]{:S(2)}) async-start(bf16[32,9,2560]{2,1,0:T(8,128)(2,1)} %all_to_all.36), calls=%async_computation.3 | async-start | bytes 5242880 | tf_op jit(solution)/shard_map/all_to_all | solution.py:205
  351.2 1.0 fusion.20
  352.2 2.9 fusion.21
  355.1 1.0 fusion.19
  357.0 1.9 gather_fusion.3
  359.8 105.0 %all-reduce.7.cloned.1.call-done = (bf16[1,16,768]{2,1,0:T(8,128)(2,1)}, bf16[1,16,768]{2,1,0:T(8,128)(2,1)}, bf16[1,768,16]{1,2,0:T(8,128)(2,1)}) async-done(((bf16[1,16,768]{2,1,0:T(8,128)(2,1)}, bf16[1,16,768]{2,1,0:T(8,128)(2,1)}, bf16[1,768,16]{1,2,0:T(8,128)(2,1)}), (bf16[1,16,768]{2,1,0:T(8,128)(2,1)}, bf16[1,16,768]{2,1,0:T(8,128)(2,1)}, bf16[1,768,16]{1,2,0:T(8,128)(2,1)})) %all-reduce.7.cloned.1.call-update) | async-done | bytes 73744 | tf_op jit(solution)/shard_map/psum | solution.py:195
  464.7 1.4 convert_element_type.180
  466.1 1.4 convert_element_type.186
  467.4 1.4 convert_element_type.189
  468.8 116.0 %all-reduce.9.cloned.1.call-done = (bf16[1,2560,16]{1,2,0:T(8,128)(2,1)}, bf16[1,2560,16]{1,2,0:T(8,128)(2,1)}, bf16[1,16,2560]{2,1,0:T(8,128)(2,1)}) async-done(((bf16[1,2560,16]{1,2,0:T(8,128)(2,1)}, bf16[1,2560,16]{1,2,0:T(8,128)(2,1)}, bf16[1,16,2560]{2,1,0:T(8,128)(2,1)}), (bf16[1,2560,16]{1,2,0:T(8,128)(2,1)}, bf16[1,2560,16]{1,2,0:T(8,128)(2,1)}, ...) | async-done | bytes 245776 | tf_op jit(solution)/shard_map/psum | solution.py:194
  584.8 1.6 convert_element_type.177
  586.4 1.6 convert_element_type.183
  587.9 1.6 convert_element_type.195
  589.5 2.0 all_to_all.38
  591.6 1.4 gather_fusion.2
  593.6 4.4 reduce_sum.34
  (126 shorter events, 16.8 us)
Async XLA Ops:
  7.2 291.5 %copy-start = (bf16[1,2560,16]{1,2,0:T(8,128)(2,1)S(1)}, bf16[1,2560,16]{1,2,0:T(8,128)(2,1)}, u32[]{:S(2)}) copy-start(bf16[1,2560,16]{1,2,0:T(8,128)(2,1)} %param.20) | copy-start | bytes 245764
  7.2 293.7 %all-gather.8.cloned.1.call-start = ((), (), s32[]{:S(2)}) async-start(), calls=%async_computation.7 | async-start | bytes 4177920 | tf_op jit(solution)/shard_map/all_gather | solution.py:161
  7.9 297.7 %all-gather.4.cloned.1.call-start = ((), (), s32[]{:S(2)}) async-start(), calls=%async_computation.5 | async-start | bytes 4177920 | tf_op jit(solution)/shard_map/all_gather | solution.py:163
  12.6 20.3 %copy-start.33 = (s32[256,1]{0,1:T(1,128)}, s32[256,1]{0,1:T(1,128)S(1)}, u32[]{:S(2)}) copy-start(s32[256,1]{0,1:T(1,128)S(1)} %compare_select_fusion) | copy-start | bytes 3076
  14.7 28.5 %all-to-all-start = ((bf16[32,9,1]{1,2,0:T(2,128)(2,1)}), bf16[32,9,1]{1,2,0:T(2,128)(2,1)S(1)}, u32[]{:S(2)}, u32[]{:S(2)}) async-start(bf16[32,9,1]{1,2,0:T(2,128)(2,1)} %all_to_all.40), calls=%async_computation | async-start | bytes 32768 | tf_op jit(solution)/shard_map/all_to_all | solution.py:153
  43.2 134.5 %copy-start.15 = (bf16[32,9,1]{1,2,0:T(2,128)(2,1)}, bf16[32,9,1]{1,2,0:T(2,128)(2,1)S(1)}, u32[]{:S(2)}) copy-start(bf16[32,9,1]{1,2,0:T(2,128)(2,1)S(1)} %all-to-all-done) | copy-start | bytes 1732
  43.2 127.1 %all-to-all-start.1 = ((bf16[32,9,2560]{2,1,0:T(8,128)(2,1)}), bf16[32,9,2560]{2,1,0:T(8,128)(2,1)S(1)}, u32[]{:S(2)}, u32[]{:S(2)}) async-start(bf16[32,9,2560]{2,1,0:T(8,128)(2,1)} %all_to_all.32), calls=%async_computation.1 | async-start | bytes 5242880 | tf_op jit(solution)/shard_map/all_to_all | solution.py:152
  170.3 126.3 %all-to-all-start.2 = ((bf16[32,9,2560]{2,1,0:T(8,128)(2,1)}), bf16[32,9,2560]{2,1,0:T(8,128)(2,1)}, u32[]{:S(2)}, u32[]{:S(2)}) async-start(bf16[32,9,2560]{2,1,0:T(8,128)(2,1)} %all_to_all.34), calls=%async_computation.2 | async-start | bytes 5242880 | tf_op jit(solution)/shard_map/all_to_all | solution.py:151
  177.0 133.3 %all-gather.6.cloned.1.call-start = ((), (), s32[]{:S(2)}) async-start(), calls=%async_computation.6 | async-start | bytes 4177920 | tf_op jit(solution)/shard_map/all_gather | solution.py:162
  184.6 114.6 %copy-start.12 = (bf16[1,2560,16]{1,2,0:T(8,128)(2,1)S(1)}, bf16[1,2560,16]{1,2,0:T(8,128)(2,1)}, u32[]{:S(2)}) copy-start(bf16[1,2560,16]{1,2,0:T(8,128)(2,1)} %param.22) | copy-start | bytes 245764
  184.6 115.7 %copy-start.4 = (bf16[288,2560]{1,0:T(8,128)(2,1)S(1)}, bf16[288,2560]{1,0:T(8,128)(2,1)}, u32[]{:S(2)}) copy-start(bf16[288,2560]{1,0:T(8,128)(2,1)} %convert_element_type.158) | copy-start | bytes 4423684
  184.6 115.7 %copy-start.13 = (bf16[1,16,2560]{2,1,0:T(8,128)(2,1)S(1)}, bf16[1,16,2560]{2,1,0:T(8,128)(2,1)}, u32[]{:S(2)}) copy-start(bf16[1,16,2560]{2,1,0:T(8,128)(2,1)} %param.25) | copy-start | bytes 245764
  299.2 5.1 copy-start.19
  300.8 8.2 %copy-start.17 = (bf16[288,16]{0,1:T(8,128)(2,1)}, bf16[288,16]{0,1:T(8,128)(2,1)S(1)}, u32[]{:S(2)}) copy-start(bf16[288,16]{0,1:T(8,128)(2,1)S(1)} %convolution_convert_fusion.2) | copy-start | bytes 27652
  300.8 3.5 copy-start.26
  305.6 3.4 copy-start.28
  310.3 3.6 copy-start.30
  310.3 3.6 copy-start.32
  310.3 3.6 copy-start.10
  310.3 3.6 copy-start.11
  313.9 0.7 copy-start.27
  314.5 5.0 copy-start.6
  314.5 13.6 %copy-start.8 = (bf16[288,768]{1,0:T(8,128)(2,1)}, bf16[288,768]{1,0:T(8,128)(2,1)S(1)}, u32[]{:S(2)}) copy-start(bf16[288,768]{1,0:T(8,128)(2,1)S(1)} %get-tuple-element.31) | copy-start | bytes 1327108
  314.6 3.3 copy-start.29
  314.6 3.5 copy-start.35
  314.8 4.7 copy-start.21
  318.1 1.4 copy-start.23
  318.1 1.9 copy-start.2
  318.1 1.8 copy-start.14
  321.4 18.3 %all-to-all-start.4 = ((bf16[32,9,1]{1,2,0:T(2,128)(2,1)}), bf16[32,9,1]{1,2,0:T(2,128)(2,1)}, u32[]{:S(2)}, u32[]{:S(2)}) async-start(bf16[32,9,1]{1,2,0:T(2,128)(2,1)} %convert_element_type.200), calls=%async_computation.4 | async-start | bytes 32768 | tf_op jit(solution)/shard_map/all_to_all | solution.py:206
  328.1 3.6 copy-start.5
  331.8 1.8 copy-start.3
  331.8 1.8 copy-start.25
  336.0 12.5 %copy-start.16 = (bf16[32,9,1]{1,2,0:T(2,128)(2,1)S(1)}, bf16[32,9,1]{1,2,0:T(2,128)(2,1)}, u32[]{:S(2)}) copy-start(bf16[32,9,1]{1,2,0:T(2,128)(2,1)} %copy-done.15) | copy-start | bytes 1732
  336.0 12.7 %copy-start.9 = (bf16[288,768]{1,0:T(8,128)(2,1)S(1)}, bf16[288,768]{1,0:T(8,128)(2,1)}, u32[]{:S(2)}) copy-start(bf16[288,768]{1,0:T(8,128)(2,1)} %copy-done.8) | copy-start | bytes 1327108
  336.0 12.7 %copy-start.20 = (bf16[288,16]{0,1:T(8,128)(2,1)S(1)}, bf16[288,16]{0,1:T(8,128)(2,1)}, u32[]{:S(2)}) copy-start(bf16[288,16]{0,1:T(8,128)(2,1)} %copy-done.19) | copy-start | bytes 27652
  336.0 13.5 %copy-start.31 = (bf16[288,16]{0,1:T(8,128)(2,1)S(1)}, bf16[288,16]{0,1:T(8,128)(2,1)}, u32[]{:S(2)}) copy-start(bf16[288,16]{0,1:T(8,128)(2,1)} %convolution_convert_fusion.1) | copy-start | bytes 27652
  336.0 14.3 %copy-start.7 = (bf16[288,768]{1,0:T(8,128)(2,1)S(1)}, bf16[288,768]{1,0:T(8,128)(2,1)}, u32[]{:S(2)}) copy-start(bf16[288,768]{1,0:T(8,128)(2,1)} %copy-done.6) | copy-start | bytes 1327108
  336.1 14.3 %copy-start.18 = (bf16[288,16]{0,1:T(8,128)(2,1)S(1)}, bf16[288,16]{0,1:T(8,128)(2,1)}, u32[]{:S(2)}) copy-start(bf16[288,16]{0,1:T(8,128)(2,1)} %copy-done.17) | copy-start | bytes 27652
  336.1 15.1 %copy-start.22 = (bf16[288,16]{0,1:T(8,128)(2,1)S(1)}, bf16[288,16]{0,1:T(8,128)(2,1)}, u32[]{:S(2)}) copy-start(bf16[288,16]{0,1:T(8,128)(2,1)} %copy-done.21) | copy-start | bytes 27652
  339.8 249.7 %all-to-all-start.3 = ((bf16[32,9,2560]{2,1,0:T(8,128)(2,1)}), bf16[32,9,2560]{2,1,0:T(8,128)(2,1)}, u32[]{:S(2)}, u32[]{:S(2)}) async-start(bf16[32,9,2560]{2,1,0:T(8,128)(2,1)} %all_to_all.36), calls=%async_computation.3 | async-start | bytes 5242880 | tf_op jit(solution)/shard_map/all_to_all | solution.py:205
  348.5 3.7 copy-start.24
  348.5 116.2 %all-reduce.7.cloned.1.call-start = ((), (), s32[]{:S(2)}) async-start(), calls=%async_computation.8 | async-start | bytes 147456 | tf_op jit(solution)/shard_map/psum | solution.py:195
  351.1 233.7 %all-reduce.9.cloned.1.call-start = ((), (), s32[]{:S(2)}) async-start(), calls=%async_computation.9 | async-start | bytes 491520 | tf_op jit(solution)/shard_map/psum | solution.py:194
  352.2 3.9 copy-start.34
  591.6 6.4 %copy-start.1 = (bf16[1,2560,16]{1,2,0:T(8,128)(2,1)S(1)}, bf16[1,2560,16]{1,2,0:T(8,128)(2,1)}, u32[]{:S(2)}) copy-start(bf16[1,2560,16]{1,2,0:T(8,128)(2,1)} %param.20) | copy-start | bytes 245764
Sparse Core Ops, SparseCore 0:
  11.0 70.9 all-gather.7
  85.0 65.4 all-gather.3
  180.8 66.4 all-gather.5
  353.2 111.5 all-reduce.6
  469.0 115.7 all-reduce.8
where the time goes:
time: 606 us; the launch traced here: 604 us
  waiting for transfers between devices  456 us (75%)
  starting transfers between devices  46.7 us (8%)
  local copies, waits for them, and re-layouts  36.2 us (6%)
  matrix products  33.9 us (6%)
  other arithmetic  17.4 us (3%)
  between operations  14.4 us (2%)
    psum x1, waiting for transfers between devices, per_device(): lax.psum(adapter_parts[0].astype(jnp.bfloat16), 'dp').astype(jnp.float32)  116 us
    all_to_all x1, waiting for transfers between devices, per_device(): lax.all_to_all(grad_send, 'expert', split_axis=0, concat_axis=0, tiled=True)  112 us
    all_to_all x1, waiting for transfers between devices, per_device(): lax.all_to_all(input_send, 'expert', split_axis=0, concat_axis=0, tiled=T...  112 us
    psum x1, waiting for transfers between devices, per_device(): lax.psum(adapter_parts[1].astype(jnp.bfloat16), 'dp').astype(jnp.float32)  105 us
    all_to_all x1, starting transfers between devices, per_device(): lax.all_to_all(weight_send.astype(jnp.bfloat16), 'expert', split_axis=0,...  16.7 us
  transfers between devices with their start and end apart: 10, of which 6 were waited for; matrix products, arithmetic and copies ran while one was open for 10% of the time, Pallas kernels for 0%

commit v1 on v0

v1 whole, which is shorter than its diff:
```python
import functools

import jax
import jax.numpy as jnp
from jax import lax
from jax.experimental import pallas as pl
from jax.experimental.pallas import tpu as pltpu
from jax.sharding import PartitionSpec as P

MESH = pl.DeviceIdType.MESH
bf16 = jnp.bfloat16
f32 = jnp.float32
i32 = jnp.int32

NE, ND = 32, 16
TD, D, F = 128, 2560, 768
H = D // 2
SH = D // ND
ROWS = 288
BW = H + 256
SCALE = 2.0


def nn(a, b):
    return lax.dot_general(a, b, (((1,), (0,)), ((), ())), preferred_element_type=f32)


def nt(a, b):
    return lax.dot_general(a, b, (((1,), (1,)), ((), ())), preferred_element_type=f32)


def tn(a, b):
    return lax.dot_general(a, b, (((0,), (0,)), ((), ())), preferred_element_type=f32)


def iota(shape, axis):
    return lax.broadcasted_iota(i32, shape, axis)


def flag(mask):
    return jnp.where(mask, 1.0, 0.0).astype(bf16)


def loop(n, body):
    def step(k, carry):
        body(k)
        return carry

    lax.fori_loop(0, n, step, 0)


def lanes(n, width=256, start=0):
    return pl.ds(pl.multiple_of(n * width + start, 128), width)


def kernel(
    tok, grd, ids, gates, wg, wu, wd, gfT, gs, ufT, us, dfT, dsec,
    tg_out, gg_out, ggi, ggo, gui, guo, gdi, gdo,
    send, recv, wbuf, sel, perm, permT, fold, unfold, x, g, sg, coef, act, hid, ggp, ugp,
    ad_send, ad_recv, ad_one, ad_all,
    s_send, s_recv, w_send, w_recv, w_own, a_send, a_recv,
):
    me = lax.axis_index("expert")
    dp = lax.axis_index("dp")

    def expert_peer(k):
        z, c = me // 2, me % 2
        m = (k + 1) // 2
        c2 = (c + (k + 1) % 2) % 2
        h = (m + 1) // 2
        dz = h * (m % 2) + (16 - h) * (1 - m % 2)
        return ((z + dz) % 16) * 2 + c2

    def dp_peer(k):
        return (dp + 1 + k) % ND

    bar = pltpu.get_barrier_semaphore()
    loop(NE - 1, lambda k: pl.semaphore_signal(
        bar, inc=1, device_id={"expert": (me + 1 + k) % NE}, device_id_type=MESH))
    loop(ND - 1, lambda k: pl.semaphore_signal(
        bar, inc=1, device_id={"dp": dp_peer(k)}, device_id_type=MESH))

    q512 = iota((512, TD), 0)
    e32 = iota((NE, TD), 0)
    id0, id1 = ids[0:1, :], ids[1:2, :]
    hot = [jnp.where(e32 == id0, 1.0, 0.0), jnp.where(e32 == id1, 1.0, 0.0)]
    earlier = flag(iota((TD, TD), 0) < iota((TD, TD), 1))
    before = nn((hot[0] + hot[1]).astype(bf16), earlier)
    slots = [jnp.sum(before * h, axis=0, keepdims=True).astype(i32) for h in hot]
    keys = [
        jnp.where(slots[0] < 8, id0 * 16 + slots[0], -16),
        jnp.where(slots[1] < 8, id1 * 16 + slots[1], -16),
    ]
    sel[:, 0:TD] = flag((q512 == keys[0]) | (q512 == keys[1]))
    sel[:, TD : 2 * TD] = flag((q512 == keys[0] + 8) | (q512 == keys[1] + 8))
    sel9 = (
        jnp.where(slots[0] == 8, hot[0], 0.0) + jnp.where(slots[1] == 8, hot[1], 0.0)
    ).astype(bf16)
    qa, qb = iota((512, 512), 0), iota((512, 512), 1)
    perm[...] = flag(qb == (qa % 16) * 32 + qa // 16)
    permT[...] = flag(qa == (qb % 16) * 32 + qb // 16)
    cb = qb % 256
    fold[...] = flag(qa == (cb // 8) * 16 + cb % 8 + (qb // 256) * 8)
    ca = qa % 256
    unfold[...] = flag(qb == (ca // 8) * 16 + ca % 8 + (qa // 256) * 8)
    put_weight = flag(iota((512, NE), 0) == iota((512, NE), 1) * 16 + 4)
    take_weight = flag(iota((NE, 512), 1) == iota((NE, 512), 0) * 16 + 4)

    def tail_to_block(buf, nine, extra):
        first = jnp.concatenate([nine[:, j * 128 : (j + 1) * 128] for j in range(16)], axis=0)
        last = jnp.concatenate([nine[:, j * 128 : (j + 1) * 128] for j in range(16, 20)], axis=0)
        send[buf, :, H : H + 128] = nn(perm[...], first).astype(bf16)
        z1 = nn(perm[:, 0:128], last)
        if extra is not None:
            z1 = z1 + nn(put_weight, extra)
        send[buf, :, H + 128 : BW] = z1.astype(bf16)

    def tail_from_block(buf):
        first = nn(permT[...], recv[buf, :, H : H + 128]).astype(bf16)
        last = nn(permT[0:128, :], recv[buf, :, H + 128 : BW]).astype(bf16)
        parts = [first[j * 32 : (j + 1) * 32] for j in range(16)]
        parts += [last[j * 32 : (j + 1) * 32] for j in range(4)]
        return parts

    def dispatch(buf, src, extra):
        def body(n):
            both = jnp.concatenate([src[:, lanes(n)], src[:, lanes(n, start=H)]], axis=0)
            send[buf, :, lanes(n)] = nn(sel[...], both).astype(bf16)

        loop(H // 256, body)
        tail_to_block(buf, nn(sel9, src[...]).astype(bf16), extra)

    def block(p):
        return pl.ds(pl.multiple_of(p * 16, 16), 16)

    def row_copy(buf, there, here):
        return pltpu.make_async_remote_copy(
            src_ref=send.at[buf, block(there)],
            dst_ref=recv.at[buf, block(here)],
            send_sem=s_send.at[buf, there],
            recv_sem=s_recv.at[buf, here],
            device_id={"expert": there},
            device_id_type=MESH,
        )

    def rows_start(buf):
        loop(NE - 1, lambda k: row_copy(buf, expert_peer(k), me).start())
        recv[buf, block(me), :] = send[buf, block(me), :]

    def rows_wait(buf):
        def body(k):
            p = (me + 1 + k) % NE
            row_copy(buf, p, p).wait_recv()

        loop(NE - 1, body)

    def rows_sent(buf):
        def body(k):
            p = (me + 1 + k) % NE
            row_copy(buf, p, p).wait_send()

        loop(NE - 1, body)

    shards = [wg, wu, wd]

    def shard_rows(p):
        return pl.ds(pl.multiple_of(p * SH, 32), SH)

    def shard_copy(t, there, here):
        return pltpu.make_async_remote_copy(
            src_ref=shards[t],
            dst_ref=wbuf.at[t, shard_rows(here)],
            send_sem=w_send.at[t, there],
            recv_sem=w_recv.at[t, here],
            device_id={"dp": there},
            device_id_type=MESH,
        )

    def own_copy(t):
        return pltpu.make_async_copy(shards[t], wbuf.at[t, shard_rows(dp)], w_own.at[t])

    def shards_start(t):
        loop(ND - 1, lambda k: shard_copy(t, dp_peer(k), dp).start())
        own_copy(t).start()

    def shards_wait(t):
        def body(k):
            p = dp_peer(k)
            shard_copy(t, p, p).wait()

        loop(ND - 1, body)
        own_copy(t).wait()

    dispatch(0, tok, None)
    pl.semaphore_wait(bar, NE - 1 + ND - 1)
    rows_start(0)
    shards_start(0)
    shards_start(1)
    shards_start(2)
    r128 = iota((128, TD), 0)
    weights = 0.0
    for k in range(2):
        a = (hot[k] * gates[k : k + 1, :]).astype(bf16)
        weights = weights + nt(a, flag(r128 == slots[k]))
    dispatch(1, grd, weights.astype(bf16))
    rows_start(1)

    def receive(buf, dst):
        def body(n):
            both = nn(unfold[...], recv[buf, :, lanes(n)]).astype(bf16)
            dst[0:256, lanes(n)] = both[0:256]
            dst[0:256, lanes(n, start=H)] = both[256:512]

        loop(H // 256, body)
        for j, part in enumerate(tail_from_block(buf)):
            dst[256:ROWS, j * 128 : (j + 1) * 128] = part

    rows_wait(0)
    receive(0, x)
    low = nt(x[...], jnp.concatenate([gfT[...], ufT[...]], axis=0)).astype(bf16)
    gate_low, up_low = low[:, 0:16], low[:, 16:32]
    shards_wait(0)
    shards_wait(1)

    def forward(n):
        c = lanes(n)
        pre = nn(x[...], wbuf[0, :, c]) + SCALE * nn(gate_low, gs[:, c])
        up = nn(x[...], wbuf[1, :, c]) + SCALE * nn(up_low, us[:, c])
        s = jax.nn.sigmoid(pre)
        a = pre * s
        act[:, c] = a
        coef[:, c] = up * s * (1.0 + pre * (1.0 - s))
        hid[:, c] = (a * up).astype(bf16)

    loop(F // 256, forward)
    hidden_low = nt(hid[...], dfT[...]).astype(bf16)

    rows_wait(1)
    receive(1, g)
    wt = nn(take_weight, recv[1, :, H + 128 : BW])
    p256 = iota((256, 128), 0)
    l256 = iota((256, 128), 1)
    spread = flag(iota((256, NE), 0) // 8 == iota((256, NE), 1))
    gather = flag(iota((NE, 256), 1) // 8 == iota((NE, 256), 0))
    diag = l256 == p256 % 8
    ninth = iota((NE, 128), 1) == 8
    w_main = jnp.sum(jnp.where(diag, nn(spread, wt.astype(bf16)), 0.0), axis=1, keepdims=True)
    w_nine = jnp.sum(jnp.where(ninth, wt, 0.0), axis=1, keepdims=True)
    weight = jnp.concatenate([w_main, w_nine], axis=0)
    u_low = nt(g[...], dsec[...])
    cot_low = (weight * u_low).astype(bf16)
    shards_wait(2)
    sg0 = SCALE * jnp.sum(hidden_low.astype(f32) * u_low, axis=1, keepdims=True)
    bgl = jnp.zeros((ROWS, 16), f32)
    bul = jnp.zeros((ROWS, 16), f32)

    def backward(n, carry):
        slot_gate, bg, bu = carry
        c = lanes(n)
        u = nn(g[...], wbuf[2, :, c])
        slot_gate = slot_gate + jnp.sum(hid[:, c].astype(f32) * u, axis=1, keepdims=True)
        hg = weight * u + SCALE * nn(cot_low, dfT[:, c])
        gg = (hg * coef[:, c]).astype(bf16)
        ug = (hg * act[:, c]).astype(bf16)
        ggp[:, c] = gg
        ugp[:, c] = ug
        return slot_gate, bg + nt(gg, gs[:, c]), bu + nt(ug, us[:, c])

    slot_gate, bgl, bul = lax.fori_loop(0, F // 256, backward, (sg0, bgl, bul))
    bgl = bgl.astype(bf16)
    bul = bul.astype(bf16)

    def slot_grad(n):
        c = pl.ds(pl.multiple_of(n * 256, 256), 256)
        value = nt(ggp[...], wbuf[0, c, :]) + nt(ugp[...], wbuf[1, c, :])
        value = value + SCALE * (nn(bgl, gfT[:, c]) + nn(bul, ufT[:, c]))
        sg[:, c] = value.astype(bf16)

    loop(D // 256, slot_grad)

    rows_sent(0)

    def pack(n):
        both = jnp.concatenate([sg[0:256, lanes(n)], sg[0:256, lanes(n, start=H)]], axis=0)
        send[2, :, lanes(n)] = nn(fold[...], both).astype(bf16)

    loop(H // 256, pack)
    back = nn(gather, jnp.where(diag, slot_gate[0:256], 0.0).astype(bf16))
    back = back + jnp.where(ninth, slot_gate[256:ROWS], 0.0)
    tail_to_block(2, sg[256:ROWS, :], back.astype(bf16))
    rows_start(2)

    bl = jnp.concatenate([bgl, bul], axis=1)

    def store4(first, value):
        for j in range(4):
            ad_send[first + j] = value[:, j * 640 : (j + 1) * 640]

    ins = (SCALE * tn(bl, x[...])).astype(bf16)
    store4(0, ins[0:16])
    store4(4, ins[16:32])
    whl = (weight * hidden_low.astype(f32)).astype(bf16)
    store4(8, (SCALE * tn(whl, g[...])).astype(bf16))
    store4(12, jnp.concatenate([
        (SCALE * tn(gate_low, ggp[...])).astype(bf16),
        (SCALE * tn(up_low, ugp[...])).astype(bf16),
        (SCALE * tn(cot_low, hid[...])).astype(bf16),
        jnp.zeros((16, 256), bf16),
    ], axis=1))

    def part_copy(phase, there, here):
        if phase == 0:
            src, dst = ad_send.at[there], ad_recv.at[here]
        else:
            src, dst = ad_one, ad_all.at[here]
        return pltpu.make_async_remote_copy(
            src_ref=src,
            dst_ref=dst,
            send_sem=a_send.at[phase, there],
            recv_sem=a_recv.at[phase, here],
            device_id={"dp": there},
            device_id_type=MESH,
        )

    def part_wait(phase):
        def body(k):
            p = dp_peer(k)
            part_copy(phase, p, p).wait()

        loop(ND - 1, body)

    loop(ND - 1, lambda k: part_copy(0, dp_peer(k), dp).start())
    ad_recv[dp] = ad_send[dp]
    part_wait(0)
    total = lax.fori_loop(
        1, ND, lambda j, t: t + ad_recv[j].astype(f32), ad_recv[0].astype(f32)
    ).astype(bf16)
    ad_one[...] = total
    loop(ND - 1, lambda k: part_copy(1, dp_peer(k), dp).start())
    ad_all[dp] = total
    part_wait(1)

    def load4(first):
        return jnp.concatenate([ad_all[first + j].astype(f32) for j in range(4)], axis=1)

    ggi[...] = load4(0)
    gui[...] = load4(4)
    gdo[...] = load4(8)
    rest = load4(12)
    ggo[...] = rest[:, 0:F]
    guo[...] = rest[:, F : 2 * F]
    gdi[...] = rest[:, 2 * F : 3 * F]

    rows_sent(1)
    rows_sent(2)
    rows_wait(2)
    nine = jnp.concatenate(tail_from_block(2), axis=1)
    sg[0:NE, :] = nine

    def combine(n):
        r = recv[2, :, lanes(n)]
        left = tn(sel[:, 0:TD], r) + tn(sel9, sg[0:NE, lanes(n)])
        right = tn(sel[:, TD : 2 * TD], r) + tn(sel9, sg[0:NE, lanes(n, start=H)])
        tg_out[:, lanes(n)] = left.astype(bf16)
        tg_out[:, lanes(n, start=H)] = right.astype(bf16)

    loop(H // 256, combine)
    wt3 = nn(take_weight, recv[2, :, H + 128 : BW]).astype(bf16)
    for k in range(2):
        picked = tn(wt3, hot[k].astype(bf16))
        gg_out[k : k + 1, :] = jnp.sum(
            jnp.where(r128 == slots[k], picked, 0.0), axis=0, keepdims=True
        )


def per_device(tokens, out_grad, expert_ids, gate_values, wg, wu, wd, gf, gs, uf, us, df, ds):
    vmem = pl.BlockSpec(memory_space=pltpu.VMEM)
    anywhere = pl.BlockSpec(memory_space=pl.ANY)
    shape = jax.ShapeDtypeStruct
    outs = pl.pallas_call(
        kernel,
        out_shape=(
            shape((TD, D), bf16),
            shape((2, TD), f32),
            shape((16, D), f32),
            shape((16, F), f32),
            shape((16, D), f32),
            shape((16, F), f32),
            shape((16, F), f32),
            shape((16, D), f32),
        ),
        in_specs=[vmem] * 4 + [anywhere] * 3 + [vmem] * 6,
        out_specs=[vmem] * 8,
        scratch_shapes=[
            pltpu.VMEM((3, 512, BW), bf16),
            pltpu.VMEM((3, 512, BW), bf16),
            pltpu.VMEM((3, D, F), bf16),
            pltpu.VMEM((512, 2 * TD), bf16),
            pltpu.VMEM((512, 512), bf16),
            pltpu.VMEM((512, 512), bf16),
            pltpu.VMEM((512, 512), bf16),
            pltpu.VMEM((512, 512), bf16),
            pltpu.VMEM((ROWS, D), bf16),
            pltpu.VMEM((ROWS, D), bf16),
            pltpu.VMEM((ROWS, D), bf16),
            pltpu.VMEM((ROWS, F), f32),
            pltpu.VMEM((ROWS, F), f32),
            pltpu.VMEM((ROWS, F), bf16),
            pltpu.VMEM((ROWS, F), bf16),
            pltpu.VMEM((ROWS, F), bf16),
            pltpu.VMEM((16, 16, 640), bf16),
            pltpu.VMEM((16, 16, 640), bf16),
            pltpu.VMEM((16, 640), bf16),
            pltpu.VMEM((16, 16, 640), bf16),
            pltpu.SemaphoreType.DMA((3, NE)),
            pltpu.SemaphoreType.DMA((3, NE)),
            pltpu.SemaphoreType.DMA((3, ND)),
            pltpu.SemaphoreType.DMA((3, ND)),
            pltpu.SemaphoreType.DMA((3,)),
            pltpu.SemaphoreType.DMA((2, ND)),
            pltpu.SemaphoreType.DMA((2, ND)),
        ],
        compiler_params=pltpu.CompilerParams(
            collective_id=0, has_side_effects=True, vmem_limit_bytes=58 * 2**20
        ),
        cost_estimate=pl.CostEstimate(
            flops=8_000_000_000, bytes_accessed=20_000_000, transcendentals=300_000
        ),
    )(
        tokens, out_grad, expert_ids.T, gate_values.T, wg[0], wu[0], wd[0],
        gf[0].T, gs[0], uf[0].T, us[0], df[0].T, ds[0],
    )
    tg, gg, ggi, ggo, gui, guo, gdi, gdo = outs
    return tg, gg.T, ggi.T[None], ggo[None], gui.T[None], guo[None], gdi.T[None], gdo[None]


def solution(mesh):
    row = P(("dp", "expert"), None)
    frozen = P("expert", "dp", None)
    one = P("expert", None, None)
    return jax.shard_map(
        per_device,
        mesh=mesh,
        in_specs=(row,) * 4 + (frozen,) * 3 + (one,) * 6,
        out_specs=(row,) * 2 + (one,) * 6,
        check_vma=False,
    )
```

time: 606 us -> 287 us (0.47)
  waiting for transfers between devices: 456 us -> 0 us
  Pallas kernels: 0 us -> 280 us
  starting transfers between devices: 46.7 us -> 0 us
  matrix products: 33.9 us -> 0 us
  local copies, waits for them, and re-layouts: 36.2 us -> 6.7 us
  other arithmetic: 17.4 us -> 0 us
  between operations: 14.4 us -> 0.67 us
    pallas_call x0 -> x1, Pallas kernels: none -> 280 us  [per_device(): pl.pallas_call(kernel, out_shape=(shape((TD, D), bf16), shape((2, TD), f3...]
    all_to_all x5 -> x0, waiting for transfers between devices: 233 us -> none  [the longest x1 112 us: per_device(): lax.all_to_all(grad_send, 'expert', split_axis=0, concat_axis=0, tiled=True)]
    psum x2 -> x0, waiting for transfers between devices: 221 us -> none  [the longest x1 116 us: per_device(): lax.psum(adapter_parts[0].astype(jnp.bfloat16), 'dp').astype(jnp.float32)]
    all_to_all x5 -> x0, starting transfers between devices: 46.3 us -> none  [the longest x1 16.7 us: per_device(): lax.all_to_all(weight_send.astype(jnp.bfloat16), 'expert', split_axis=0,...]
    dot_general x24 -> x0, matrix products: 33.9 us -> none  [the longest x9 11.8 us: right_operand_flipped(): lax.dot_general(left, right, (((1,), (1,)), ((), ())), preferred_element_...]
    convert_element_type x12 -> x0, other arithmetic: 11.6 us -> none  [the longest x1 2.02 us: expert_adapter_rows(): (row_weighting[:, None] * grad_wide).astype(jnp.bfloat16)]
    gather x5 -> x0, local copies, waits for them, and re-layouts: 9.62 us -> none  [the longest x1 3.1 us: per_device(): input_send = jnp.concatenate([tokens, blank], axis=0)[source]]
    all_to_all x5 -> x0, local copies, waits for them, and re-layouts: 9.38 us -> none  [the longest x2 3.9 us: per_device(): lax.all_to_all(grad_back, 'expert', split_axis=0, concat_axis=0, tiled=True)]
  transfers between devices with their start and end apart: 10 -> 0, of which waited for: 6 -> 0; matrix products, arithmetic and copies ran while one was open for 10% -> 0% of each run, Pallas kernels for 0% -> 0%
where the time goes in v1:
time: 287 us
  Pallas kernels  280 us (98%)
  local copies, waits for them, and re-layouts  6.7 us (2%)
    pallas_call x1, Pallas kernels, per_device(): pl.pallas_call(kernel, out_shape=(shape((TD, D), bf16), shape((2, TD), f3...  280 us
    unnamed x22, local copies, waits for them, and re-layouts  6.7 us

profile of v1, /device:TPU:1, one launch (start us, length us, event | category | flops | bytes accessed | tf_op | source)
XLA Modules:
  0.0 287.1 jit_solution(8984834262243717059)
XLA Ops:
  0.6 279.7 %shard_map.188 = (bf16[128,2560]{1,0:T(8,128)(2,1)}, f32[2,128]{1,0:T(2,128)}, f32[16,2560]{1,0:T(8,128)}, f32[16,768]{1,0:T(8,128)}, f32[16,2560]{1,0:T(8,128)}...) custom-call(bf16[128,2560]{1,0:T(8,128)(2,1)} %tok.1, bf16[128,2560]{1,0:T(8,128)(2,1)} %grd.1, ...), custom_call_target="tpu_custom_call" | custom-call | flops 8000000000 | bytes 20000000 | tf_op jit(solution)/shard_map/pallas_call | solution.py:380
  280.4 0.0 copy-start.6
  280.4 0.0 copy-start.2
  280.4 2.0 copy.29
  282.4 0.0 copy-done.6
  282.4 0.6 copy.30
  283.0 0.0 copy-done.2
  283.0 0.0 copy-start.5
  283.0 0.0 copy-start.1
  283.0 0.7 copy.31
  283.6 0.1 copy-done.5
  283.8 0.6 copy.32
  284.4 0.0 copy-done.1
  284.4 0.0 copy-start.4
  284.4 0.0 copy-start.3
  284.4 0.7 copy.33
  285.1 0.1 copy-done.4
  285.2 0.0 copy-start
  285.2 0.6 copy.34
  285.8 0.0 copy-done.3
  285.8 0.6 copy.35
  286.4 0.0 copy-done
  286.4 0.7 copy.36
Async XLA Ops:
  280.4 2.0 copy-start.6
  280.4 2.6 copy-start.2
  283.0 0.8 copy-start.5
  283.0 1.4 copy-start.1
  284.4 0.8 copy-start.4
  284.4 1.4 copy-start.3
  285.2 1.2 copy-start

commit v2 on v1

--- a/solution.py
+++ b/solution.py
@@ -54,31 +54,56 @@
 
 
 def kernel(
-    tok, grd, ids, gates, wg, wu, wd, gfT, gs, ufT, us, dfT, dsec,
+    tok, grd, ids, gates, wg, wu, wd, in_gf, in_gs, in_uf, in_us, in_df, in_ds,
     tg_out, gg_out, ggi, ggo, gui, guo, gdi, gdo,
     send, recv, wbuf, sel, perm, permT, fold, unfold, x, g, sg, coef, act, hid, ggp, ugp,
-    ad_send, ad_recv, ad_one, ad_all,
-    s_send, s_recv, w_send, w_recv, w_own, a_send, a_recv,
+    ad_send, ad_recv, ad_one, ad_all, ad_far, ad_near,
+    gfT, ufT, dsec, gs, us, dfT, moved, packed, ad_moved, ad_buf,
+    s_send, s_recv, m_send, m_recv, x_send, x_recv, x_own,
+    y1_send, y1_recv, y2_send, y2_recv, a_send, a_recv, f_send, f_recv,
 ):
     me = lax.axis_index("expert")
     dp = lax.axis_index("dp")
 
-    def expert_peer(k):
-        z, c = me // 2, me % 2
-        m = (k + 1) // 2
-        c2 = (c + (k + 1) % 2) % 2
-        h = (m + 1) // 2
-        dz = h * (m % 2) + (16 - h) * (1 - m % 2)
-        return ((z + dz) % 16) * 2 + c2
+    z, c = me // 2, me % 2
+    y, xx = dp // 4, dp % 4
+    b = dp % 2
+    odd = (b + c) % 2
+
+    mine = ((z + 16 + b * (14 * c - 7)) % 16) * 2 + c
+    my_slot = b * 16 + (3 + odd) * 2 + c
+    my_k = c + 2 * b + 4 * (3 + odd)
+    z_to = (z + 23 - 14 * c) % 16
+    z_from = (z + 9 + 14 * c) % 16
+
+    def home(k):
+        c2, b2, j = k % 2, (k // 2) % 2, k // 4
+        zp = (z + 13 + j - (b2 + c2) % 2) % 16
+        expert = ((zp + 16 + b2 * (14 * c2 - 7)) % 16) * 2 + c2
+        return dp - b + b2, zp * 2 + c2, expert, b * 16 + j * 2 + c
+
+    def origin(slot):
+        cs, j, bs = slot % 2, (slot % 16) // 2, slot // 16
+        zs = (z + 19 - j + odd) % 16
+        return dp - b + bs, zs * 2 + cs
 
     def dp_peer(k):
         return (dp + 1 + k) % ND
 
     bar = pltpu.get_barrier_semaphore()
-    loop(NE - 1, lambda k: pl.semaphore_signal(
-        bar, inc=1, device_id={"expert": (me + 1 + k) % NE}, device_id_type=MESH))
-    loop(ND - 1, lambda k: pl.semaphore_signal(
-        bar, inc=1, device_id={"dp": dp_peer(k)}, device_id_type=MESH))
+
+    def greet(d, e):
+        pl.semaphore_signal(
+            bar, inc=1, device_id={"dp": d, "expert": e}, device_id_type=MESH)
+
+    def greet_rows(k):
+        i = (2 * b + c + 16 + 1 + k) % 36
+        greet(dp - b + (i // 2) % 2, ((z + 12 + i // 4) % 16) * 2 + i % 2)
+
+    loop(35, greet_rows)
+    greet(dp, z_to * 2 + c)
+    greet(dp, z_from * 2 + c)
+    loop(ND - 1, lambda k: greet(dp_peer(k), me))
 
     q512 = iota((512, TD), 0)
     e32 = iota((NE, TD), 0)
@@ -133,70 +158,148 @@
     def block(p):
         return pl.ds(pl.multiple_of(p * 16, 16), 16)
 
-    def row_copy(buf, there, here):
+    def row_copy(buf, src, dst, d, e):
         return pltpu.make_async_remote_copy(
-            src_ref=send.at[buf, block(there)],
-            dst_ref=recv.at[buf, block(here)],
-            send_sem=s_send.at[buf, there],
-            recv_sem=s_recv.at[buf, here],
-            device_id={"expert": there},
+            src_ref=send.at[buf, block(src)],
+            dst_ref=recv.at[buf, block(dst)],
+            send_sem=s_send.at[buf, src],
+            recv_sem=s_recv.at[buf, dst],
+            device_id={"dp": d, "expert": e},
             device_id_type=MESH,
         )
 
     def rows_start(buf):
-        loop(NE - 1, lambda k: row_copy(buf, expert_peer(k), me).start())
-        recv[buf, block(me), :] = send[buf, block(me), :]
-
-    def rows_wait(buf):
-        def body(k):
-            p = (me + 1 + k) % NE
-            row_copy(buf, p, p).wait_recv()
+        def body(i):
+            d, e, expert, slot = home((my_k + 1 + i) % NE)
+            row_copy(buf, expert, slot, d, e).start()
 
         loop(NE - 1, body)
-
-    def rows_sent(buf):
-        def body(k):
-            p = (me + 1 + k) % NE
-            row_copy(buf, p, p).wait_send()
+        recv[buf, block(my_slot), :] = send[buf, block(mine), :]
+
+    def rows_back():
+        def body(i):
+            slot = (my_slot + 1 + i) % NE
+            d, e = origin(slot)
+            row_copy(2, slot, mine, d, e).start()
 
         loop(NE - 1, body)
-
-    shards = [wg, wu, wd]
-
-    def shard_rows(p):
-        return pl.ds(pl.multiple_of(p * SH, 32), SH)
-
-    def shard_copy(t, there, here):
+        recv[2, block(mine), :] = send[2, block(my_slot), :]
+
+    def rows_wait(buf, own):
+        loop(NE - 1, lambda i: row_copy(
+            buf, (own + 1 + i) % NE, (own + 1 + i) % NE, dp, z_to * 2 + c).wait_recv())
+
+    def rows_sent(buf, own):
+        loop(NE - 1, lambda i: row_copy(
+            buf, (own + 1 + i) % NE, (own + 1 + i) % NE, dp, z_to * 2 + c).wait_send())
+
+    shards = [wg, wu, wd, packed.at[dp]]
+    second = [moved.at[0], moved.at[1], moved.at[2], ad_moved]
+    order = (3, 0, 1, 2)
+
+    def shard(t, d):
+        if t == 3:
+            return ad_buf.at[d]
+        return wbuf.at[t, pl.ds(pl.multiple_of(d * SH, 32), SH)]
+
+    def four(t, row, part):
+        if t == 3:
+            return ad_buf.at[pl.ds(row * 4 + (2 if part == 2 else 0), 2 if part else 4)]
+        first = row * 4 * SH + (2 * SH if part == 2 else 0)
+        return wbuf.at[t, pl.ds(pl.multiple_of(first, 64), (2 if part else 4) * SH)]
+
+    def move(t):
         return pltpu.make_async_remote_copy(
-            src_ref=shards[t],
-            dst_ref=wbuf.at[t, shard_rows(here)],
-            send_sem=w_send.at[t, there],
-            recv_sem=w_recv.at[t, here],
-            device_id={"dp": there},
-            device_id_type=MESH,
+            src_ref=shards[t], dst_ref=second[t], send_sem=m_send.at[t], recv_sem=m_recv.at[t],
+            device_id={"expert": z_to * 2 + c}, device_id_type=MESH,
         )
 
-    def own_copy(t):
-        return pltpu.make_async_copy(shards[t], wbuf.at[t, shard_rows(dp)], w_own.at[t])
-
-    def shards_start(t):
-        loop(ND - 1, lambda k: shard_copy(t, dp_peer(k), dp).start())
-        own_copy(t).start()
-
-    def shards_wait(t):
-        def body(k):
-            p = dp_peer(k)
-            shard_copy(t, p, p).wait()
-
-        loop(ND - 1, body)
-        own_copy(t).wait()
+    def along_x(t, src, to, at):
+        return pltpu.make_async_remote_copy(
+            src_ref=src, dst_ref=shard(t, y * 4 + at),
+            send_sem=x_send.at[t, to], recv_sem=x_recv.at[t, at],
+            device_id={"dp": y * 4 + to}, device_id_type=MESH,
+        )
+
+    def x_start(t, stream):
+        src = shards[t] if stream == 0 else second[t]
+
+        def body(i):
+            to = stream + 2 * i
+
+            @pl.when(to != xx)
+            def _():
+                along_x(t, src, to, xx).start()
+
+            @pl.when(to == xx)
+            def _():
+                pltpu.make_async_copy(src, shard(t, dp), x_own.at[t]).start()
+
+        loop(2, body)
+
+    def x_wait(t):
+        loop(3, lambda i: along_x(
+            t, shards[t], (xx + 1 + i) % 4, (xx + 1 + i) % 4).wait_recv())
+        pltpu.make_async_copy(shards[t], shard(t, dp), x_own.at[t]).wait()
+
+    def x_sent(t):
+        loop(3, lambda i: along_x(
+            t, shards[t], (xx + 1 + i) % 4, (xx + 1 + i) % 4).wait_send())
+
+    ends = ((y + 1) % 4, (y + 3) % 4)
+
+    def along_y(t, way, hop):
+        region = four(t, y, 0) if hop == 1 else four(t, ends[1 - way], way + 1)
+        sems = (y1_send, y1_recv) if hop == 1 else (y2_send, y2_recv)
+        return pltpu.make_async_remote_copy(
+            src_ref=region, dst_ref=region,
+            send_sem=sems[0].at[t, way], recv_sem=sems[1].at[t, way],
+            device_id={"dp": ends[way] * 4 + xx}, device_id_type=MESH,
+        )
+
+    def landed_y(t, way, hop):
+        region = four(t, ends[1 - way], 0) if hop == 1 else four(t, (y + 2) % 4, way + 1)
+        sems = (y1_send, y1_recv) if hop == 1 else (y2_send, y2_recv)
+        pltpu.make_async_remote_copy(
+            src_ref=region, dst_ref=region,
+            send_sem=sems[0].at[t, way], recv_sem=sems[1].at[t, way],
+            device_id={"dp": ends[way] * 4 + xx}, device_id_type=MESH,
+        ).wait_recv()
+
+    def move_done(t):
+        move(t).wait_recv()
+        x_start(t, 1)
+
+    def y_first(t):
+        x_wait(t)
+        along_y(t, 0, 1).start()
+        along_y(t, 1, 1).start()
+
+    def y_second(t):
+        for way in range(2):
+            landed_y(t, way, 1)
+            along_y(t, way, 2).start()
+
+    def y_done(t):
+        landed_y(t, 0, 2)
+        landed_y(t, 1, 2)
+
+    for first, ref in ((0, in_gf), (4, in_uf), (8, in_ds)):
+        for j in range(4):
+            packed[first + j] = ref[:, j * 640 : (j + 1) * 640]
+    small = jnp.concatenate(
+        [in_gs[...], in_us[...], in_df[...], jnp.zeros((16, 256), bf16)], axis=1
+    )
+    for j in range(4):
+        packed[12 + j] = small[:, j * 640 : (j + 1) * 640]
 
     dispatch(0, tok, None)
-    pl.semaphore_wait(bar, NE - 1 + ND - 1)
+    pl.semaphore_wait(bar, 35 + 2 + ND - 1)
+    for t in order:
+        move(t).start()
+    for t in order:
+        x_start(t, 0)
     rows_start(0)
-    shards_start(0)
-    shards_start(1)
-    shards_start(2)
     r128 = iota((128, TD), 0)
     weights = 0.0
     for k in range(2):
@@ -205,6 +308,18 @@
     dispatch(1, grd, weights.astype(bf16))
     rows_start(1)
 
+    move_done(3)
+    move_done(0)
+    y_first(3)
+    y_first(0)
+    move_done(1)
+    y_first(1)
+    y_second(3)
+    y_second(0)
+    move_done(2)
+    y_first(2)
+    y_second(1)
+
     def receive(buf, dst):
         def body(n):
             both = nn(unfold[...], recv[buf, :, lanes(n)]).astype(bf16)
@@ -215,12 +330,25 @@
         for j, part in enumerate(tail_from_block(buf)):
             dst[256:ROWS, j * 128 : (j + 1) * 128] = part
 
-    rows_wait(0)
+    rows_wait(0, my_slot)
     receive(0, x)
+    y_done(3)
+
+    def load4(buf, first):
+        return jnp.concatenate([buf[first + j] for j in range(4)], axis=1)
+
+    gfT[...] = load4(ad_buf, 0)
+    ufT[...] = load4(ad_buf, 4)
+    dsec[...] = load4(ad_buf, 8)
+    rest = load4(ad_buf, 12)
+    gs[...] = rest[:, 0:F]
+    us[...] = rest[:, F : 2 * F]
+    dfT[...] = rest[:, 2 * F : 3 * F]
     low = nt(x[...], jnp.concatenate([gfT[...], ufT[...]], axis=0)).astype(bf16)
     gate_low, up_low = low[:, 0:16], low[:, 16:32]
-    shards_wait(0)
-    shards_wait(1)
+    y_second(2)
+    y_done(0)
+    y_done(1)
 
     def forward(n):
         c = lanes(n)
@@ -235,7 +363,7 @@
     loop(F // 256, forward)
     hidden_low = nt(hid[...], dfT[...]).astype(bf16)
 
-    rows_wait(1)
+    rows_wait(1, my_slot)
     receive(1, g)
     wt = nn(take_weight, recv[1, :, H + 128 : BW])
     p256 = iota((256, 128), 0)
@@ -249,7 +377,7 @@
     weight = jnp.concatenate([w_main, w_nine], axis=0)
     u_low = nt(g[...], dsec[...])
     cot_low = (weight * u_low).astype(bf16)
-    shards_wait(2)
+    y_done(2)
     sg0 = SCALE * jnp.sum(hidden_low.astype(f32) * u_low, axis=1, keepdims=True)
     bgl = jnp.zeros((ROWS, 16), f32)
     bul = jnp.zeros((ROWS, 16), f32)
@@ -278,8 +406,6 @@
 
     loop(D // 256, slot_grad)
 
-    rows_sent(0)
-
     def pack(n):
         both = jnp.concatenate([sg[0:256, lanes(n)], sg[0:256, lanes(n, start=H)]], axis=0)
         send[2, :, lanes(n)] = nn(fold[...], both).astype(bf16)
@@ -288,7 +414,7 @@
     back = nn(gather, jnp.where(diag, slot_gate[0:256], 0.0).astype(bf16))
     back = back + jnp.where(ninth, slot_gate[256:ROWS], 0.0)
     tail_to_block(2, sg[256:ROWS, :], back.astype(bf16))
-    rows_start(2)
+    rows_back()
 
     bl = jnp.concatenate([bgl, bul], axis=1)
 
@@ -332,28 +458,43 @@
     loop(ND - 1, lambda k: part_copy(0, dp_peer(k), dp).start())
     ad_recv[dp] = ad_send[dp]
     part_wait(0)
-    total = lax.fori_loop(
-        1, ND, lambda j, t: t + ad_recv[j].astype(f32), ad_recv[0].astype(f32)
-    ).astype(bf16)
+
+    def both(j, t):
+        return t[0] + ad_recv[2 * j].astype(f32), t[1] + ad_recv[2 * j + 1].astype(f32)
+
+    zero = jnp.zeros((16, 640), f32)
+    here, there = lax.fori_loop(0, ND // 2, both, (zero, zero))
+    ad_far[...] = there
+    far = pltpu.make_async_remote_copy(
+        src_ref=ad_far, dst_ref=ad_near, send_sem=f_send.at[0], recv_sem=f_recv.at[0],
+        device_id={"expert": z_from * 2 + c}, device_id_type=MESH,
+    )
+    far.start()
+    far.wait()
+    total = (here + ad_near[...]).astype(bf16)
     ad_one[...] = total
     loop(ND - 1, lambda k: part_copy(1, dp_peer(k), dp).start())
     ad_all[dp] = total
     part_wait(1)
 
-    def load4(first):
-        return jnp.concatenate([ad_all[first + j].astype(f32) for j in range(4)], axis=1)
-
-    ggi[...] = load4(0)
-    gui[...] = load4(4)
-    gdo[...] = load4(8)
-    rest = load4(12)
+    ggi[...] = load4(ad_all, 0).astype(f32)
+    gui[...] = load4(ad_all, 4).astype(f32)
+    gdo[...] = load4(ad_all, 8).astype(f32)
+    rest = load4(ad_all, 12).astype(f32)
     ggo[...] = rest[:, 0:F]
     guo[...] = rest[:, F : 2 * F]
     gdi[...] = rest[:, 2 * F : 3 * F]
 
-    rows_sent(1)
-    rows_sent(2)
-    rows_wait(2)
+    for t in order:
+        move(t).wait_send()
+        x_sent(t)
+        for way in range(2):
+            along_y(t, way, 1).wait_send()
+            along_y(t, way, 2).wait_send()
+    rows_sent(0, mine)
+    rows_sent(1, mine)
+    rows_sent(2, my_slot)
+    rows_wait(2, mine)
     nine = jnp.concatenate(tail_from_block(2), axis=1)
     sg[0:NE, :] = nine
 
@@ -412,13 +553,33 @@
             pltpu.VMEM((16, 16, 640), bf16),
             pltpu.VMEM((16, 640), bf16),
             pltpu.VMEM((16, 16, 640), bf16),
+            pltpu.VMEM((16, 640), f32),
+            pltpu.VMEM((16, 640), f32),
+            pltpu.VMEM((16, D), bf16),
+            pltpu.VMEM((16, D), bf16),
+            pltpu.VMEM((16, D), bf16),
+            pltpu.VMEM((16, F), bf16),
+            pltpu.VMEM((16, F), bf16),
+            pltpu.VMEM((16, F), bf16),
+            pltpu.VMEM((3, SH, F), bf16),
+            pltpu.VMEM((16, 16, 640), bf16),
+            pltpu.VMEM((16, 640), bf16),
+            pltpu.VMEM((16, 16, 640), bf16),
             pltpu.SemaphoreType.DMA((3, NE)),
             pltpu.SemaphoreType.DMA((3, NE)),
-            pltpu.SemaphoreType.DMA((3, ND)),
-            pltpu.SemaphoreType.DMA((3, ND)),
-            pltpu.SemaphoreType.DMA((3,)),
+            pltpu.SemaphoreType.DMA((4,)),
+            pltpu.SemaphoreType.DMA((4,)),
+            pltpu.SemaphoreType.DMA((4, 4)),
+            pltpu.SemaphoreType.DMA((4, 4)),
+            pltpu.SemaphoreType.DMA((4,)),
+            pltpu.SemaphoreType.DMA((4, 2)),
+            pltpu.SemaphoreType.DMA((4, 2)),
+            pltpu.SemaphoreType.DMA((4, 2)),
+            pltpu.SemaphoreType.DMA((4, 2)),
             pltpu.SemaphoreType.DMA((2, ND)),
             pltpu.SemaphoreType.DMA((2, ND)),
+            pltpu.SemaphoreType.DMA((1,)),
+            pltpu.SemaphoreType.DMA((1,)),
         ],
         compiler_params=pltpu.CompilerParams(
             collective_id=0, has_side_effects=True, vmem_limit_bytes=58 * 2**20

time: 287 us -> 232 us (0.81)
  the two profiles are of different devices: /device:TPU:1 before, /device:TPU:102 now
where the time goes in v2:
time: 232 us
  Pallas kernels  224 us (97%)
  local copies, waits for them, and re-layouts  6.7 us (3%)
    pallas_call x1, Pallas kernels, per_device(): pl.pallas_call(kernel, out_shape=(shape((TD, D), bf16), shape((2, TD), f3...  224 us
    unnamed x22, local copies, waits for them, and re-layouts  6.7 us

profile of v2, /device:TPU:102, one launch (start us, length us, event | category | flops | bytes accessed | tf_op | source)
XLA Modules:
  0.0 231.8 jit_solution(4008790758978494357)
XLA Ops:
  0.6 224.4 %shard_map.188 = (bf16[128,2560]{1,0:T(8,128)(2,1)}, f32[2,128]{1,0:T(2,128)}, f32[16,2560]{1,0:T(8,128)}, f32[16,768]{1,0:T(8,128)}, f32[16,2560]{1,0:T(8,128)}...) custom-call(bf16[128,2560]{1,0:T(8,128)(2,1)} %tok.1, bf16[128,2560]{1,0:T(8,128)(2,1)} %grd.1, ...), custom_call_target="tpu_custom_call" | custom-call | flops 8000000000 | bytes 20000000 | tf_op jit(solution)/shard_map/pallas_call | solution.py:521
  225.1 0.0 copy-start.6
  225.1 0.0 copy-start.2
  225.1 2.0 copy.29
  227.1 0.0 copy-done.6
  227.1 0.6 copy.30
  227.6 0.0 copy-done.2
  227.7 0.0 copy-start.5
  227.7 0.0 copy-start.1
  227.7 0.7 copy.31
  228.3 0.1 copy-done.5
  228.4 0.6 copy.32
  229.1 0.0 copy-done.1
  229.1 0.0 copy-start.4
  229.1 0.0 copy-start.3
  229.1 0.7 copy.33
  229.7 0.1 copy-done.4
  229.9 0.0 copy-start
  229.9 0.6 copy.34
  230.5 0.0 copy-done.3
  230.5 0.6 copy.35
  231.1 0.0 copy-done
  231.1 0.7 copy.36
Async XLA Ops:
  225.1 2.0 copy-start.6
  225.1 2.6 %copy-start.2 = (f32[16,2560]{1,0:T(8,128)S(1)}, f32[16,2560]{1,0:T(8,128)}, u32[]{:S(2)}) copy-start(f32[16,2560]{1,0:T(8,128)} %get-tuple-element.18) | copy-start | bytes 491524
  227.7 0.8 copy-start.5
  227.7 1.4 copy-start.1
  229.1 0.8 copy-start.4
  229.1 1.4 copy-start.3
  229.9 1.2 copy-start

commit v3 on v2

--- a/solution.py
+++ b/solution.py
@@ -18,6 +18,7 @@
 SH = D // ND
 ROWS = 288
 BW = H + 256
+PIECES = 9
 SCALE = 2.0
 
 
@@ -58,8 +59,8 @@
     tg_out, gg_out, ggi, ggo, gui, guo, gdi, gdo,
     send, recv, wbuf, sel, perm, permT, fold, unfold, x, g, sg, coef, act, hid, ggp, ugp,
     ad_send, ad_recv, ad_one, ad_all, ad_far, ad_near,
-    gfT, ufT, dsec, gs, us, dfT, moved, packed, ad_moved, ad_buf,
-    s_send, s_recv, m_send, m_recv, x_send, x_recv, x_own,
+    gfT, ufT, dsec, gs, us, dfT, staged, moved, packed, ad_moved, ad_buf,
+    s_send, s_recv, st_sem, m_send, m_recv, x_send, x_recv, x_own,
     y1_send, y1_recv, y2_send, y2_recv, a_send, a_recv, f_send, f_recv,
 ):
     me = lax.axis_index("expert")
@@ -193,24 +194,39 @@
         loop(NE - 1, lambda i: row_copy(
             buf, (own + 1 + i) % NE, (own + 1 + i) % NE, dp, z_to * 2 + c).wait_send())
 
-    shards = [wg, wu, wd, packed.at[dp]]
-    second = [moved.at[0], moved.at[1], moved.at[2], ad_moved]
-    order = (3, 0, 1, 2)
+    AD = PIECES
+
+    def stage(t):
+        ref, n = ((wg, wu)[t % 2], t // 2) if t < 6 else (wd, t - 6)
+        return pltpu.make_async_copy(
+            ref.at[:, n * 256 : (n + 1) * 256], staged.at[t], st_sem.at[t])
+
+    for t in range(PIECES):
+        stage(t).start()
+
+    def is_ad(t):
+        return isinstance(t, int) and t == AD
+
+    def first_of(t):
+        return packed.at[dp] if is_ad(t) else staged.at[t]
+
+    def second_of(t):
+        return ad_moved if is_ad(t) else moved.at[t]
 
     def shard(t, d):
-        if t == 3:
+        if is_ad(t):
             return ad_buf.at[d]
         return wbuf.at[t, pl.ds(pl.multiple_of(d * SH, 32), SH)]
 
     def four(t, row, part):
-        if t == 3:
+        if is_ad(t):
             return ad_buf.at[pl.ds(row * 4 + (2 if part == 2 else 0), 2 if part else 4)]
         first = row * 4 * SH + (2 * SH if part == 2 else 0)
         return wbuf.at[t, pl.ds(pl.multiple_of(first, 64), (2 if part else 4) * SH)]
 
     def move(t):
         return pltpu.make_async_remote_copy(
-            src_ref=shards[t], dst_ref=second[t], send_sem=m_send.at[t], recv_sem=m_recv.at[t],
+            src_ref=first_of(t), dst_ref=second_of(t), send_sem=m_send.at[t], recv_sem=m_recv.at[t],
             device_id={"expert": z_to * 2 + c}, device_id_type=MESH,
         )
 
@@ -222,7 +238,7 @@
         )
 
     def x_start(t, stream):
-        src = shards[t] if stream == 0 else second[t]
+        src = first_of(t) if stream == 0 else second_of(t)
 
         def body(i):
             to = stream + 2 * i
@@ -239,12 +255,12 @@
 
     def x_wait(t):
         loop(3, lambda i: along_x(
-            t, shards[t], (xx + 1 + i) % 4, (xx + 1 + i) % 4).wait_recv())
-        pltpu.make_async_copy(shards[t], shard(t, dp), x_own.at[t]).wait()
+            t, first_of(t), (xx + 1 + i) % 4, (xx + 1 + i) % 4).wait_recv())
+        pltpu.make_async_copy(first_of(t), shard(t, dp), x_own.at[t]).wait()
 
     def x_sent(t):
         loop(3, lambda i: along_x(
-            t, shards[t], (xx + 1 + i) % 4, (xx + 1 + i) % 4).wait_send())
+            t, first_of(t), (xx + 1 + i) % 4, (xx + 1 + i) % 4).wait_send())
 
     ends = ((y + 1) % 4, (y + 3) % 4)
 
@@ -295,10 +311,12 @@
 
     dispatch(0, tok, None)
     pl.semaphore_wait(bar, 35 + 2 + ND - 1)
-    for t in order:
-        move(t).start()
-    for t in order:
-        x_start(t, 0)
+    for t in range(PIECES):
+        stage(t).wait()
+    move(AD).start()
+    loop(PIECES, lambda t: move(t).start())
+    x_start(AD, 0)
+    loop(PIECES, lambda t: x_start(t, 0))
     rows_start(0)
     r128 = iota((128, TD), 0)
     weights = 0.0
@@ -308,17 +326,20 @@
     dispatch(1, grd, weights.astype(bf16))
     rows_start(1)
 
-    move_done(3)
+    move_done(AD)
     move_done(0)
-    y_first(3)
+    y_first(AD)
+    move_done(1)
     y_first(0)
-    move_done(1)
-    y_first(1)
-    y_second(3)
-    y_second(0)
-    move_done(2)
-    y_first(2)
-    y_second(1)
+    y_second(AD)
+
+    def relay(i):
+        move_done(i + 2)
+        y_first(i + 1)
+        y_second(i)
+
+    loop(PIECES - 2, relay)
+    y_first(PIECES - 1)
 
     def receive(buf, dst):
         def body(n):
@@ -332,7 +353,7 @@
 
     rows_wait(0, my_slot)
     receive(0, x)
-    y_done(3)
+    y_done(AD)
 
     def load4(buf, first):
         return jnp.concatenate([buf[first + j] for j in range(4)], axis=1)
@@ -346,14 +367,15 @@
     dfT[...] = rest[:, 2 * F : 3 * F]
     low = nt(x[...], jnp.concatenate([gfT[...], ufT[...]], axis=0)).astype(bf16)
     gate_low, up_low = low[:, 0:16], low[:, 16:32]
-    y_second(2)
-    y_done(0)
-    y_done(1)
+    y_second(PIECES - 2)
+    y_second(PIECES - 1)
 
     def forward(n):
         c = lanes(n)
-        pre = nn(x[...], wbuf[0, :, c]) + SCALE * nn(gate_low, gs[:, c])
-        up = nn(x[...], wbuf[1, :, c]) + SCALE * nn(up_low, us[:, c])
+        y_done(2 * n)
+        pre = nn(x[...], wbuf[2 * n]) + SCALE * nn(gate_low, gs[:, c])
+        y_done(2 * n + 1)
+        up = nn(x[...], wbuf[2 * n + 1]) + SCALE * nn(up_low, us[:, c])
         s = jax.nn.sigmoid(pre)
         a = pre * s
         act[:, c] = a
@@ -377,7 +399,6 @@
     weight = jnp.concatenate([w_main, w_nine], axis=0)
     u_low = nt(g[...], dsec[...])
     cot_low = (weight * u_low).astype(bf16)
-    y_done(2)
     sg0 = SCALE * jnp.sum(hidden_low.astype(f32) * u_low, axis=1, keepdims=True)
     bgl = jnp.zeros((ROWS, 16), f32)
     bul = jnp.zeros((ROWS, 16), f32)
@@ -385,7 +406,8 @@
     def backward(n, carry):
         slot_gate, bg, bu = carry
         c = lanes(n)
-        u = nn(g[...], wbuf[2, :, c])
+        y_done(6 + n)
+        u = nn(g[...], wbuf[6 + n])
         slot_gate = slot_gate + jnp.sum(hid[:, c].astype(f32) * u, axis=1, keepdims=True)
         hg = weight * u + SCALE * nn(cot_low, dfT[:, c])
         gg = (hg * coef[:, c]).astype(bf16)
@@ -397,24 +419,6 @@
     slot_gate, bgl, bul = lax.fori_loop(0, F // 256, backward, (sg0, bgl, bul))
     bgl = bgl.astype(bf16)
     bul = bul.astype(bf16)
-
-    def slot_grad(n):
-        c = pl.ds(pl.multiple_of(n * 256, 256), 256)
-        value = nt(ggp[...], wbuf[0, c, :]) + nt(ugp[...], wbuf[1, c, :])
-        value = value + SCALE * (nn(bgl, gfT[:, c]) + nn(bul, ufT[:, c]))
-        sg[:, c] = value.astype(bf16)
-
-    loop(D // 256, slot_grad)
-
-    def pack(n):
-        both = jnp.concatenate([sg[0:256, lanes(n)], sg[0:256, lanes(n, start=H)]], axis=0)
-        send[2, :, lanes(n)] = nn(fold[...], both).astype(bf16)
-
-    loop(H // 256, pack)
-    back = nn(gather, jnp.where(diag, slot_gate[0:256], 0.0).astype(bf16))
-    back = back + jnp.where(ninth, slot_gate[256:ROWS], 0.0)
-    tail_to_block(2, sg[256:ROWS, :], back.astype(bf16))
-    rows_back()
 
     bl = jnp.concatenate([bgl, bul], axis=1)
 
@@ -457,6 +461,18 @@
 
     loop(ND - 1, lambda k: part_copy(0, dp_peer(k), dp).start())
     ad_recv[dp] = ad_send[dp]
+
+    def slot_grad(n):
+        c = pl.ds(pl.multiple_of(n * 256, 256), 256)
+        value = SCALE * (nn(bgl, gfT[:, c]) + nn(bul, ufT[:, c]))
+        for k in range(3):
+            f = slice(k * 256, (k + 1) * 256)
+            value = value + nt(ggp[:, f], wbuf[2 * k, c, :])
+            value = value + nt(ugp[:, f], wbuf[2 * k + 1, c, :])
+        sg[:, c] = value.astype(bf16)
+
+    loop(D // 256, slot_grad)
+
     part_wait(0)
 
     def both(j, t):
@@ -470,6 +486,17 @@
         device_id={"expert": z_from * 2 + c}, device_id_type=MESH,
     )
     far.start()
+
+    def pack(n):
+        both = jnp.concatenate([sg[0:256, lanes(n)], sg[0:256, lanes(n, start=H)]], axis=0)
+        send[2, :, lanes(n)] = nn(fold[...], both).astype(bf16)
+
+    loop(H // 256, pack)
+    back = nn(gather, jnp.where(diag, slot_gate[0:256], 0.0).astype(bf16))
+    back = back + jnp.where(ninth, slot_gate[256:ROWS], 0.0)
+    tail_to_block(2, sg[256:ROWS, :], back.astype(bf16))
+    rows_back()
+
     far.wait()
     total = (here + ad_near[...]).astype(bf16)
     ad_one[...] = total
@@ -485,12 +512,16 @@
     guo[...] = rest[:, F : 2 * F]
     gdi[...] = rest[:, 2 * F : 3 * F]
 
-    for t in order:
+
+    def all_sent(t):
         move(t).wait_send()
         x_sent(t)
         for way in range(2):
             along_y(t, way, 1).wait_send()
             along_y(t, way, 2).wait_send()
+
+    all_sent(AD)
+    loop(PIECES, all_sent)
     rows_sent(0, mine)
     rows_sent(1, mine)
     rows_sent(2, my_slot)
@@ -535,7 +566,7 @@
         scratch_shapes=[
             pltpu.VMEM((3, 512, BW), bf16),
             pltpu.VMEM((3, 512, BW), bf16),
-            pltpu.VMEM((3, D, F), bf16),
+            pltpu.VMEM((PIECES, D, 256), bf16),
             pltpu.VMEM((512, 2 * TD), bf16),
             pltpu.VMEM((512, 512), bf16),
             pltpu.VMEM((512, 512), bf16),
@@ -561,21 +592,23 @@
             pltpu.VMEM((16, F), bf16),
             pltpu.VMEM((16, F), bf16),
             pltpu.VMEM((16, F), bf16),
-            pltpu.VMEM((3, SH, F), bf16),
+            pltpu.VMEM((PIECES, SH, 256), bf16),
+            pltpu.VMEM((PIECES, SH, 256), bf16),
             pltpu.VMEM((16, 16, 640), bf16),
             pltpu.VMEM((16, 640), bf16),
             pltpu.VMEM((16, 16, 640), bf16),
             pltpu.SemaphoreType.DMA((3, NE)),
             pltpu.SemaphoreType.DMA((3, NE)),
-            pltpu.SemaphoreType.DMA((4,)),
-            pltpu.SemaphoreType.DMA((4,)),
-            pltpu.SemaphoreType.DMA((4, 4)),
-            pltpu.SemaphoreType.DMA((4, 4)),
-            pltpu.SemaphoreType.DMA((4,)),
-            pltpu.SemaphoreType.DMA((4, 2)),
-            pltpu.SemaphoreType.DMA((4, 2)),
-            pltpu.SemaphoreType.DMA((4, 2)),
-            pltpu.SemaphoreType.DMA((4, 2)),
+            pltpu.SemaphoreType.DMA((PIECES,)),
+            pltpu.SemaphoreType.DMA((PIECES + 1,)),
+            pltpu.SemaphoreType.DMA((PIECES + 1,)),
+            pltpu.SemaphoreType.DMA((PIECES + 1, 4)),
+            pltpu.SemaphoreType.DMA((PIECES + 1, 4)),
+            pltpu.SemaphoreType.DMA((PIECES + 1,)),
+            pltpu.SemaphoreType.DMA((PIECES + 1, 2)),
+            pltpu.SemaphoreType.DMA((PIECES + 1, 2)),
+            pltpu.SemaphoreType.DMA((PIECES + 1, 2)),
+            pltpu.SemaphoreType.DMA((PIECES + 1, 2)),
             pltpu.SemaphoreType.DMA((2, ND)),
             pltpu.SemaphoreType.DMA((2, ND)),
             pltpu.SemaphoreType.DMA((1,)),

time: 232 us -> 213 us (0.918)
  the two profiles are of different devices: /device:TPU:102 before, /device:TPU:1 now
where the time goes in v3:
time: 213 us; the launch traced here: 212 us
  Pallas kernels  205 us (96%)
  local copies, waits for them, and re-layouts  6.7 us (3%)
    pallas_call x1, Pallas kernels, per_device(): pl.pallas_call(kernel, out_shape=(shape((TD, D), bf16), shape((2, TD), f3...  205 us
    unnamed x22, local copies, waits for them, and re-layouts  6.7 us

profile of v3, /device:TPU:1, one launch (start us, length us, event | category | flops | bytes accessed | tf_op | source)
XLA Modules:
  0.0 212.3 jit_solution(17302447910002675800)
XLA Ops:
  0.6 205.0 %shard_map.188 = (bf16[128,2560]{1,0:T(8,128)(2,1)}, f32[2,128]{1,0:T(2,128)}, f32[16,2560]{1,0:T(8,128)}, f32[16,768]{1,0:T(8,128)}, f32[16,2560]{1,0:T(8,128)}...) custom-call(bf16[128,2560]{1,0:T(8,128)(2,1)} %tok.1, bf16[128,2560]{1,0:T(8,128)(2,1)} %grd.1, ...), custom_call_target="tpu_custom_call" | custom-call | flops 8000000000 | bytes 20000000 | tf_op jit(solution)/shard_map/pallas_call | solution.py:552
  205.6 0.0 copy-start.6
  205.6 0.0 copy-start.2
  205.6 2.0 copy.29
  207.6 0.0 copy-done.6
  207.6 0.6 copy.30
  208.2 0.0 copy-done.2
  208.2 0.0 copy-start.5
  208.2 0.0 copy-start.1
  208.2 0.7 copy.31
  208.9 0.1 copy-done.5
  209.0 0.6 copy.32
  209.6 0.0 copy-done.1
  209.6 0.0 copy-start.4
  209.6 0.0 copy-start.3
  209.6 0.7 copy.33
  210.3 0.1 copy-done.4
  210.4 0.0 copy-start
  210.4 0.6 copy.34
  211.0 0.0 copy-done.3
  211.0 0.6 copy.35
  211.7 0.0 copy-done
  211.7 0.7 copy.36
Async XLA Ops:
  205.6 2.0 copy-start.6
  205.6 2.6 %copy-start.2 = (f32[16,2560]{1,0:T(8,128)S(1)}, f32[16,2560]{1,0:T(8,128)}, u32[]{:S(2)}) copy-start(f32[16,2560]{1,0:T(8,128)} %get-tuple-element.18) | copy-start | bytes 491524
  208.2 0.8 copy-start.5
  208.2 1.4 copy-start.1
  209.6 0.8 copy-start.4
  209.6 1.4 copy-start.3
  210.4 1.2 copy-start

commit v4 on v3

v4 whole, which is shorter than its diff:
```python
import functools

import jax
import jax.numpy as jnp
from jax import lax
from jax.experimental import pallas as pl
from jax.experimental.pallas import tpu as pltpu
from jax.sharding import PartitionSpec as P

MESH = pl.DeviceIdType.MESH
bf16 = jnp.bfloat16
f32 = jnp.float32
i32 = jnp.int32

NE, ND = 32, 16
TD, D, F = 128, 2560, 768
H = D // 2
SH = D // ND
ROWS = 288
BW = H + 256
PIECES = 9
SCALE = 2.0


def nn(a, b):
    return lax.dot_general(a, b, (((1,), (0,)), ((), ())), preferred_element_type=f32)


def nt(a, b):
    return lax.dot_general(a, b, (((1,), (1,)), ((), ())), preferred_element_type=f32)


def tn(a, b):
    return lax.dot_general(a, b, (((0,), (0,)), ((), ())), preferred_element_type=f32)


def iota(shape, axis):
    return lax.broadcasted_iota(i32, shape, axis)


def flag(mask):
    return jnp.where(mask, 1.0, 0.0).astype(bf16)


def loop(n, body):
    def step(k, carry):
        body(k)
        return carry

    lax.fori_loop(0, n, step, 0)


def lanes(n, width=256, start=0):
    return pl.ds(pl.multiple_of(n * width + start, 128), width)


def pair_slots(ids):
    e32 = iota((NE, TD), 0)
    id0, id1 = ids[0:1, :], ids[1:2, :]
    hot = [jnp.where(e32 == id0, 1.0, 0.0), jnp.where(e32 == id1, 1.0, 0.0)]
    earlier = flag(iota((TD, TD), 0) < iota((TD, TD), 1))
    before = nn((hot[0] + hot[1]).astype(bf16), earlier)
    slots = [jnp.sum(before * h, axis=0, keepdims=True).astype(i32) for h in hot]
    sel9 = (
        jnp.where(slots[0] == 8, hot[0], 0.0) + jnp.where(slots[1] == 8, hot[1], 0.0)
    ).astype(bf16)
    return id0, id1, hot, slots, sel9


def kernel(
    tok, grd, ids, gates, wg, wu, wd, in_gf, in_gs, in_uf, in_us, in_df, in_ds,
    block_out, sel_out, perm_out, ad_out,
    send, recv, wbuf, sel, perm, permT, fold, unfold, x, g, sg, coef, act, hid, ggp, ugp,
    ad_send, ad_recv, ad_one, ad_all, ad_far, ad_near,
    gfT, ufT, dsec, gs, us, dfT, staged, moved, packed, ad_moved, ad_buf,
    s_send, s_recv, st_sem, m_send, m_recv, x_send, x_recv, x_own,
    y1_send, y1_recv, y2_send, y2_recv, a_send, a_recv, f_send, f_recv, o_sem,
):
    me = lax.axis_index("expert")
    dp = lax.axis_index("dp")

    z, c = me // 2, me % 2
    y, xx = dp // 4, dp % 4
    b = dp % 2
    odd = (b + c) % 2

    mine = ((z + 16 + b * (14 * c - 7)) % 16) * 2 + c
    my_slot = b * 16 + (3 + odd) * 2 + c
    my_k = c + 2 * b + 4 * (3 + odd)
    z_to = (z + 23 - 14 * c) % 16
    z_from = (z + 9 + 14 * c) % 16

    def home(k):
        c2, b2, j = k % 2, (k // 2) % 2, k // 4
        zp = (z + 13 + j - (b2 + c2) % 2) % 16
        expert = ((zp + 16 + b2 * (14 * c2 - 7)) % 16) * 2 + c2
        return dp - b + b2, zp * 2 + c2, expert, b * 16 + j * 2 + c

    def origin(slot):
        cs, j, bs = slot % 2, (slot % 16) // 2, slot // 16
        zs = (z + 19 - j + odd) % 16
        return dp - b + bs, zs * 2 + cs

    def dp_peer(k):
        return (dp + 1 + k) % ND

    bar = pltpu.get_barrier_semaphore()

    def greet(d, e):
        pl.semaphore_signal(
            bar, inc=1, device_id={"dp": d, "expert": e}, device_id_type=MESH)

    def greet_rows(k):
        i = (2 * b + c + 16 + 1 + k) % 36
        greet(dp - b + (i // 2) % 2, ((z + 12 + i // 4) % 16) * 2 + i % 2)

    loop(35, greet_rows)
    greet(dp, z_to * 2 + c)
    greet(dp, z_from * 2 + c)
    loop(ND - 1, lambda k: greet(dp_peer(k), me))

    def block(p):
        return pl.ds(pl.multiple_of(p * 16, 16), 16)

    def row_copy(buf, src, dst, d, e):
        return pltpu.make_async_remote_copy(
            src_ref=send.at[buf, block(src)],
            dst_ref=recv.at[buf, block(dst)],
            send_sem=s_send.at[buf, src],
            recv_sem=s_recv.at[buf, dst],
            device_id={"dp": d, "expert": e},
            device_id_type=MESH,
        )

    def rows_start(buf):
        def body(i):
            d, e, expert, slot = home((my_k + 1 + i) % NE)
            row_copy(buf, expert, slot, d, e).start()

        loop(NE - 1, body)
        recv[buf, block(my_slot), :] = send[buf, block(mine), :]

    CUT = 512

    def back_copy(part, src, dst, d, e):
        c = pl.ds(0, CUT) if part == 0 else pl.ds(CUT, BW - CUT)
        return pltpu.make_async_remote_copy(
            src_ref=send.at[2, block(src), c],
            dst_ref=recv.at[2, block(dst), c],
            send_sem=s_send.at[2 + part, src],
            recv_sem=s_recv.at[2 + part, dst],
            device_id={"dp": d, "expert": e},
            device_id_type=MESH,
        )

    def rows_back(part):
        def body(i):
            slot = (my_slot + 1 + i) % NE
            d, e = origin(slot)
            back_copy(part, slot, mine, d, e).start()

        loop(NE - 1, body)
        c = slice(0, CUT) if part == 0 else slice(CUT, BW)
        recv[2, block(mine), c] = send[2, block(my_slot), c]

    def back_wait(part):
        loop(NE - 1, lambda i: back_copy(
            part, (mine + 1 + i) % NE, (mine + 1 + i) % NE, dp, z_to * 2 + c).wait_recv())

    def back_sent(part):
        loop(NE - 1, lambda i: back_copy(
            part, (my_slot + 1 + i) % NE, (my_slot + 1 + i) % NE, dp, z_to * 2 + c).wait_send())

    def rows_wait(buf, own):
        loop(NE - 1, lambda i: row_copy(
            buf, (own + 1 + i) % NE, (own + 1 + i) % NE, dp, z_to * 2 + c).wait_recv())

    def rows_sent(buf, own):
        loop(NE - 1, lambda i: row_copy(
            buf, (own + 1 + i) % NE, (own + 1 + i) % NE, dp, z_to * 2 + c).wait_send())

    AD = PIECES

    def stage(t):
        ref, n = ((wg, wu)[t % 2], t // 2) if t < 6 else (wd, t - 6)
        return pltpu.make_async_copy(
            ref.at[:, n * 256 : (n + 1) * 256], staged.at[t], st_sem.at[t])

    for t in range(PIECES):
        stage(t).start()

    def is_ad(t):
        return isinstance(t, int) and t == AD

    def first_of(t):
        return packed.at[dp] if is_ad(t) else staged.at[t]

    def second_of(t):
        return ad_moved if is_ad(t) else moved.at[t]

    def shard(t, d):
        if is_ad(t):
            return ad_buf.at[d]
        return wbuf.at[t, pl.ds(pl.multiple_of(d * SH, 32), SH)]

    def four(t, row, part):
        if is_ad(t):
            return ad_buf.at[pl.ds(row * 4 + (2 if part == 2 else 0), 2 if part else 4)]
        first = row * 4 * SH + (2 * SH if part == 2 else 0)
        return wbuf.at[t, pl.ds(pl.multiple_of(first, 64), (2 if part else 4) * SH)]

    def move(t):
        return pltpu.make_async_remote_copy(
            src_ref=first_of(t), dst_ref=second_of(t), send_sem=m_send.at[t], recv_sem=m_recv.at[t],
            device_id={"expert": z_to * 2 + c}, device_id_type=MESH,
        )

    def along_x(t, src, to, at):
        return pltpu.make_async_remote_copy(
            src_ref=src, dst_ref=shard(t, y * 4 + at),
            send_sem=x_send.at[t, to], recv_sem=x_recv.at[t, at],
            device_id={"dp": y * 4 + to}, device_id_type=MESH,
        )

    def x_start(t, stream):
        src = first_of(t) if stream == 0 else second_of(t)

        def body(i):
            to = stream + 2 * i

            @pl.when(to != xx)
            def _():
                along_x(t, src, to, xx).start()

            @pl.when(to == xx)
            def _():
                pltpu.make_async_copy(src, shard(t, dp), x_own.at[t]).start()

        loop(2, body)

    def x_wait(t):
        loop(3, lambda i: along_x(
            t, first_of(t), (xx + 1 + i) % 4, (xx + 1 + i) % 4).wait_recv())
        pltpu.make_async_copy(first_of(t), shard(t, dp), x_own.at[t]).wait()

    def x_sent(t):
        loop(3, lambda i: along_x(
            t, first_of(t), (xx + 1 + i) % 4, (xx + 1 + i) % 4).wait_send())

    ends = ((y + 1) % 4, (y + 3) % 4)

    def along_y(t, way, hop):
        region = four(t, y, 0) if hop == 1 else four(t, ends[1 - way], way + 1)
        sems = (y1_send, y1_recv) if hop == 1 else (y2_send, y2_recv)
        return pltpu.make_async_remote_copy(
            src_ref=region, dst_ref=region,
            send_sem=sems[0].at[t, way], recv_sem=sems[1].at[t, way],
            device_id={"dp": ends[way] * 4 + xx}, device_id_type=MESH,
        )

    def landed_y(t, way, hop):
        region = four(t, ends[1 - way], 0) if hop == 1 else four(t, (y + 2) % 4, way + 1)
        sems = (y1_send, y1_recv) if hop == 1 else (y2_send, y2_recv)
        pltpu.make_async_remote_copy(
            src_ref=region, dst_ref=region,
            send_sem=sems[0].at[t, way], recv_sem=sems[1].at[t, way],
            device_id={"dp": ends[way] * 4 + xx}, device_id_type=MESH,
        ).wait_recv()

    def move_done(t):
        move(t).wait_recv()
        x_start(t, 1)

    def y_first(t):
        x_wait(t)
        along_y(t, 0, 1).start()
        along_y(t, 1, 1).start()

    def y_second(t):
        for way in range(2):
            landed_y(t, way, 1)
            along_y(t, way, 2).start()

    def y_done(t):
        landed_y(t, 0, 2)
        landed_y(t, 1, 2)

    for first, ref in ((0, in_gf), (4, in_uf), (8, in_ds)):
        for j in range(4):
            packed[first + j] = ref[:, j * 640 : (j + 1) * 640]
    small = jnp.concatenate(
        [in_gs[...], in_us[...], in_df[...], jnp.zeros((16, 256), bf16)], axis=1
    )
    for j in range(4):
        packed[12 + j] = small[:, j * 640 : (j + 1) * 640]

    for t in range(PIECES):
        stage(t).wait()
    pl.semaphore_wait(bar, 35 + 2 + ND - 1)
    move(AD).start()
    loop(PIECES, lambda t: move(t).start())
    x_start(AD, 0)
    loop(PIECES, lambda t: x_start(t, 0))

    id0, id1, hot, slots, sel9 = pair_slots(ids)
    q512 = iota((512, TD), 0)
    keys = [
        jnp.where(slots[0] < 8, id0 * 16 + slots[0], -16),
        jnp.where(slots[1] < 8, id1 * 16 + slots[1], -16),
    ]
    sel[:, 0:TD] = flag((q512 == keys[0]) | (q512 == keys[1]))
    sel[:, TD : 2 * TD] = flag((q512 == keys[0] + 8) | (q512 == keys[1] + 8))
    qa, qb = iota((512, 512), 0), iota((512, 512), 1)
    perm[...] = flag(qb == (qa % 16) * 32 + qa // 16)
    permT[...] = flag(qa == (qb % 16) * 32 + qb // 16)
    cb = qb % 256
    fold[...] = flag(qa == (cb // 8) * 16 + cb % 8 + (qb // 256) * 8)
    ca = qa % 256
    unfold[...] = flag(qb == (ca // 8) * 16 + ca % 8 + (qa // 256) * 8)
    put_weight = flag(iota((512, NE), 0) == iota((512, NE), 1) * 16 + 4)
    take_weight = flag(iota((NE, 512), 1) == iota((NE, 512), 0) * 16 + 4)


    def tail_to_block(buf, nine, extra):
        first = jnp.concatenate([nine[:, j * 128 : (j + 1) * 128] for j in range(16)], axis=0)
        last = jnp.concatenate([nine[:, j * 128 : (j + 1) * 128] for j in range(16, 20)], axis=0)
        send[buf, :, H : H + 128] = nn(perm[...], first).astype(bf16)
        z1 = nn(perm[:, 0:128], last)
        if extra is not None:
            z1 = z1 + nn(put_weight, extra)
        send[buf, :, H + 128 : BW] = z1.astype(bf16)

    def tail_from_block(buf):
        first = nn(permT[...], recv[buf, :, H : H + 128]).astype(bf16)
        last = nn(permT[0:128, :], recv[buf, :, H + 128 : BW]).astype(bf16)
        parts = [first[j * 32 : (j + 1) * 32] for j in range(16)]
        parts += [last[j * 32 : (j + 1) * 32] for j in range(4)]
        return parts

    def dispatch(buf, src, extra):
        def body(n):
            both = jnp.concatenate([src[:, lanes(n)], src[:, lanes(n, start=H)]], axis=0)
            send[buf, :, lanes(n)] = nn(sel[...], both).astype(bf16)

        loop(H // 256, body)
        tail_to_block(buf, nn(sel9, src[...]).astype(bf16), extra)

    dispatch(0, tok, None)
    rows_start(0)
    sel_copy = pltpu.make_async_copy(sel, sel_out, o_sem.at[0])
    sel_copy.start()
    perm_copy = pltpu.make_async_copy(permT, perm_out, o_sem.at[1])
    perm_copy.start()
    r128 = iota((128, TD), 0)
    weights = 0.0
    for k in range(2):
        a = (hot[k] * gates[k : k + 1, :]).astype(bf16)
        weights = weights + nt(a, flag(r128 == slots[k]))
    dispatch(1, grd, weights.astype(bf16))
    rows_start(1)

    move_done(AD)
    move_done(0)
    y_first(AD)
    move_done(1)
    y_first(0)
    y_second(AD)

    def relay(i):
        move_done(i + 2)
        y_first(i + 1)
        y_second(i)

    loop(PIECES - 2, relay)
    y_first(PIECES - 1)

    def receive(buf, dst):
        def body(n):
            both = nn(unfold[...], recv[buf, :, lanes(n)]).astype(bf16)
            dst[0:256, lanes(n)] = both[0:256]
            dst[0:256, lanes(n, start=H)] = both[256:512]

        loop(H // 256, body)
        for j, part in enumerate(tail_from_block(buf)):
            dst[256:ROWS, j * 128 : (j + 1) * 128] = part

    rows_wait(0, my_slot)
    receive(0, x)
    y_done(AD)

    def load4(buf, first):
        return jnp.concatenate([buf[first + j] for j in range(4)], axis=1)

    gfT[...] = load4(ad_buf, 0)
    ufT[...] = load4(ad_buf, 4)
    dsec[...] = load4(ad_buf, 8)
    rest = load4(ad_buf, 12)
    gs[...] = rest[:, 0:F]
    us[...] = rest[:, F : 2 * F]
    dfT[...] = rest[:, 2 * F : 3 * F]
    low = nt(x[...], jnp.concatenate([gfT[...], ufT[...]], axis=0)).astype(bf16)
    gate_low, up_low = low[:, 0:16], low[:, 16:32]
    y_second(PIECES - 2)
    y_second(PIECES - 1)

    def forward(n):
        c = lanes(n)
        y_done(2 * n)
        pre = nn(x[...], wbuf[2 * n]) + SCALE * nn(gate_low, gs[:, c])
        y_done(2 * n + 1)
        up = nn(x[...], wbuf[2 * n + 1]) + SCALE * nn(up_low, us[:, c])
        s = jax.nn.sigmoid(pre)
        a = pre * s
        act[:, c] = a
        coef[:, c] = up * s * (1.0 + pre * (1.0 - s))
        hid[:, c] = (a * up).astype(bf16)

    loop(F // 256, forward)
    hidden_low = nt(hid[...], dfT[...]).astype(bf16)

    rows_wait(1, my_slot)
    receive(1, g)
    wt = nn(take_weight, recv[1, :, H + 128 : BW])
    p256 = iota((256, 128), 0)
    l256 = iota((256, 128), 1)
    spread = flag(iota((256, NE), 0) // 8 == iota((256, NE), 1))
    gather = flag(iota((NE, 256), 1) // 8 == iota((NE, 256), 0))
    diag = l256 == p256 % 8
    ninth = iota((NE, 128), 1) == 8
    w_main = jnp.sum(jnp.where(diag, nn(spread, wt.astype(bf16)), 0.0), axis=1, keepdims=True)
    w_nine = jnp.sum(jnp.where(ninth, wt, 0.0), axis=1, keepdims=True)
    weight = jnp.concatenate([w_main, w_nine], axis=0)
    u_low = nt(g[...], dsec[...])
    cot_low = (weight * u_low).astype(bf16)
    sg0 = SCALE * jnp.sum(hidden_low.astype(f32) * u_low, axis=1, keepdims=True)
    bgl = jnp.zeros((ROWS, 16), f32)
    bul = jnp.zeros((ROWS, 16), f32)

    def backward(n, carry):
        slot_gate, bg, bu = carry
        c = lanes(n)
        y_done(6 + n)
        u = nn(g[...], wbuf[6 + n])
        slot_gate = slot_gate + jnp.sum(hid[:, c].astype(f32) * u, axis=1, keepdims=True)
        hg = weight * u + SCALE * nn(cot_low, dfT[:, c])
        gg = (hg * coef[:, c]).astype(bf16)
        ug = (hg * act[:, c]).astype(bf16)
        ggp[:, c] = gg
        ugp[:, c] = ug
        return slot_gate, bg + nt(gg, gs[:, c]), bu + nt(ug, us[:, c])

    slot_gate, bgl, bul = lax.fori_loop(0, F // 256, backward, (sg0, bgl, bul))
    bgl = bgl.astype(bf16)
    bul = bul.astype(bf16)

    def slot_grad(n):
        c = pl.ds(pl.multiple_of(n * 256, 256), 256)
        value = SCALE * (nn(bgl, gfT[:, c]) + nn(bul, ufT[:, c]))
        for k in range(3):
            f = slice(k * 256, (k + 1) * 256)
            value = value + nt(ggp[:, f], wbuf[2 * k, c, :])
            value = value + nt(ugp[:, f], wbuf[2 * k + 1, c, :])
        sg[:, c] = value.astype(bf16)

    def pack(n):
        both = jnp.concatenate([sg[0:256, lanes(n)], sg[0:256, lanes(n, start=H)]], axis=0)
        send[2, :, lanes(n)] = nn(fold[...], both).astype(bf16)

    def both_halves(n):
        slot_grad(n)
        slot_grad(n + H // 256)
        pack(n)

    loop(CUT // 256, both_halves)
    rows_back(0)

    bl = jnp.concatenate([bgl, bul], axis=1)

    def store4(first, value):
        for j in range(4):
            ad_send[first + j] = value[:, j * 640 : (j + 1) * 640]

    ins = (SCALE * tn(bl, x[...])).astype(bf16)
    store4(0, ins[0:16])
    store4(4, ins[16:32])
    whl = (weight * hidden_low.astype(f32)).astype(bf16)
    store4(8, (SCALE * tn(whl, g[...])).astype(bf16))
    store4(12, jnp.concatenate([
        (SCALE * tn(gate_low, ggp[...])).astype(bf16),
        (SCALE * tn(up_low, ugp[...])).astype(bf16),
        (SCALE * tn(cot_low, hid[...])).astype(bf16),
        jnp.zeros((16, 256), bf16),
    ], axis=1))

    def part_copy(phase, there, here):
        if phase == 0:
            src, dst = ad_send.at[there], ad_recv.at[here]
        else:
            src, dst = ad_one, ad_all.at[here]
        return pltpu.make_async_remote_copy(
            src_ref=src,
            dst_ref=dst,
            send_sem=a_send.at[phase, there],
            recv_sem=a_recv.at[phase, here],
            device_id={"dp": there},
            device_id_type=MESH,
        )

    def part_wait(phase):
        def body(k):
            p = dp_peer(k)
            part_copy(phase, p, p).wait()

        loop(ND - 1, body)

    loop(ND - 1, lambda k: part_copy(0, dp_peer(k), dp).start())
    ad_recv[dp] = ad_send[dp]

    loop(H // 256 - CUT // 256, lambda n: both_halves(n + CUT // 256))
    back = nn(gather, jnp.where(diag, slot_gate[0:256], 0.0).astype(bf16))
    back = back + jnp.where(ninth, slot_gate[256:ROWS], 0.0)
    tail_to_block(2, sg[256:ROWS, :], back.astype(bf16))
    part_wait(0)

    def both(j, t):
        return t[0] + ad_recv[2 * j].astype(f32), t[1] + ad_recv[2 * j + 1].astype(f32)

    zero = jnp.zeros((16, 640), f32)
    here, there = lax.fori_loop(0, ND // 2, both, (zero, zero))
    ad_far[...] = there
    far = pltpu.make_async_remote_copy(
        src_ref=ad_far, dst_ref=ad_near, send_sem=f_send.at[0], recv_sem=f_recv.at[0],
        device_id={"expert": z_from * 2 + c}, device_id_type=MESH,
    )
    far.start()
    rows_back(1)

    far.wait()
    total = (here + ad_near[...]).astype(bf16)
    ad_one[...] = total
    loop(ND - 1, lambda k: part_copy(1, dp_peer(k), dp).start())
    ad_all[dp] = total
    part_wait(1)

    ad_copy = pltpu.make_async_copy(ad_all, ad_out, o_sem.at[2])
    ad_copy.start()

    def all_sent(t):
        move(t).wait_send()
        x_sent(t)
        for way in range(2):
            along_y(t, way, 1).wait_send()
            along_y(t, way, 2).wait_send()

    all_sent(AD)
    loop(PIECES, all_sent)
    rows_sent(0, mine)
    rows_sent(1, mine)
    back_sent(0)
    back_sent(1)
    back_wait(0)
    back_wait(1)
    block_copy = pltpu.make_async_copy(recv.at[2], block_out, o_sem.at[3])
    block_copy.start()
    for copy in (sel_copy, perm_copy, ad_copy, block_copy):
        copy.wait()


def combine_kernel(
    blocks, sel, permT, sums, ids, tg_out, gg_out, ggi, ggo, gui, guo, gdi, gdo, sg
):
    _, _, hot, slots, sel9 = pair_slots(ids)
    first = nn(permT[...], blocks[:, H : H + 128]).astype(bf16)
    last = nn(permT[0:128, :], blocks[:, H + 128 : BW]).astype(bf16)
    for j in range(16):
        sg[:, j * 128 : (j + 1) * 128] = first[j * 32 : (j + 1) * 32]
    for j in range(4):
        sg[:, (16 + j) * 128 : (17 + j) * 128] = last[j * 32 : (j + 1) * 32]

    def combine(n):
        r = blocks[:, lanes(n)]
        left = tn(sel[:, 0:TD], r) + tn(sel9, sg[:, lanes(n)])
        right = tn(sel[:, TD : 2 * TD], r) + tn(sel9, sg[:, lanes(n, start=H)])
        tg_out[:, lanes(n)] = left.astype(bf16)
        tg_out[:, lanes(n, start=H)] = right.astype(bf16)

    loop(H // 256, combine)
    take_weight = flag(iota((NE, 512), 1) == iota((NE, 512), 0) * 16 + 4)
    r128 = iota((128, TD), 0)
    wt3 = nn(take_weight, blocks[:, H + 128 : BW]).astype(bf16)
    for k in range(2):
        picked = tn(wt3, hot[k].astype(bf16))
        gg_out[k : k + 1, :] = jnp.sum(
            jnp.where(r128 == slots[k], picked, 0.0), axis=0, keepdims=True
        )

    def load4(first):
        return jnp.concatenate([sums[first + j] for j in range(4)], axis=1).astype(f32)

    ggi[...] = load4(0)
    gui[...] = load4(4)
    gdo[...] = load4(8)
    rest = load4(12)
    ggo[...] = rest[:, 0:F]
    guo[...] = rest[:, F : 2 * F]
    gdi[...] = rest[:, 2 * F : 3 * F]


def per_device(tokens, out_grad, expert_ids, gate_values, wg, wu, wd, gf, gs, uf, us, df, ds):
    vmem = pl.BlockSpec(memory_space=pltpu.VMEM)
    anywhere = pl.BlockSpec(memory_space=pl.ANY)
    shape = jax.ShapeDtypeStruct
    blocks, sel, permT, sums = pl.pallas_call(
        kernel,
        out_shape=(
            shape((512, BW), bf16),
            shape((512, 2 * TD), bf16),
            shape((512, 512), bf16),
            shape((16, 16, 640), bf16),
        ),
        in_specs=[vmem] * 4 + [anywhere] * 3 + [vmem] * 6,
        out_specs=[anywhere] * 4,
        scratch_shapes=[
            pltpu.VMEM((3, 512, BW), bf16),
            pltpu.VMEM((3, 512, BW), bf16),
            pltpu.VMEM((PIECES, D, 256), bf16),
            pltpu.VMEM((512, 2 * TD), bf16),
            pltpu.VMEM((512, 512), bf16),
            pltpu.VMEM((512, 512), bf16),
            pltpu.VMEM((512, 512), bf16),
            pltpu.VMEM((512, 512), bf16),
            pltpu.VMEM((ROWS, D), bf16),
            pltpu.VMEM((ROWS, D), bf16),
            pltpu.VMEM((ROWS, D), bf16),
            pltpu.VMEM((ROWS, F), f32),
            pltpu.VMEM((ROWS, F), f32),
            pltpu.VMEM((ROWS, F), bf16),
            pltpu.VMEM((ROWS, F), bf16),
            pltpu.VMEM((ROWS, F), bf16),
            pltpu.VMEM((16, 16, 640), bf16),
            pltpu.VMEM((16, 16, 640), bf16),
            pltpu.VMEM((16, 640), bf16),
            pltpu.VMEM((16, 16, 640), bf16),
            pltpu.VMEM((16, 640), f32),
            pltpu.VMEM((16, 640), f32),
            pltpu.VMEM((16, D), bf16),
            pltpu.VMEM((16, D), bf16),
            pltpu.VMEM((16, D), bf16),
            pltpu.VMEM((16, F), bf16),
            pltpu.VMEM((16, F), bf16),
            pltpu.VMEM((16, F), bf16),
            pltpu.VMEM((PIECES, SH, 256), bf16),
            pltpu.VMEM((PIECES, SH, 256), bf16),
            pltpu.VMEM((16, 16, 640), bf16),
            pltpu.VMEM((16, 640), bf16),
            pltpu.VMEM((16, 16, 640), bf16),
            pltpu.SemaphoreType.DMA((4, NE)),
            pltpu.SemaphoreType.DMA((4, NE)),
            pltpu.SemaphoreType.DMA((PIECES,)),
            pltpu.SemaphoreType.DMA((PIECES + 1,)),
            pltpu.SemaphoreType.DMA((PIECES + 1,)),
            pltpu.SemaphoreType.DMA((PIECES + 1, 4)),
            pltpu.SemaphoreType.DMA((PIECES + 1, 4)),
            pltpu.SemaphoreType.DMA((PIECES + 1,)),
            pltpu.SemaphoreType.DMA((PIECES + 1, 2)),
            pltpu.SemaphoreType.DMA((PIECES + 1, 2)),
            pltpu.SemaphoreType.DMA((PIECES + 1, 2)),
            pltpu.SemaphoreType.DMA((PIECES + 1, 2)),
            pltpu.SemaphoreType.DMA((2, ND)),
            pltpu.SemaphoreType.DMA((2, ND)),
            pltpu.SemaphoreType.DMA((1,)),
            pltpu.SemaphoreType.DMA((1,)),
            pltpu.SemaphoreType.DMA((4,)),
        ],
        compiler_params=pltpu.CompilerParams(
            collective_id=0, has_side_effects=True, vmem_limit_bytes=58 * 2**20
        ),
        cost_estimate=pl.CostEstimate(
            flops=8_000_000_000, bytes_accessed=20_000_000, transcendentals=300_000
        ),
    )(
        tokens, out_grad, expert_ids.T, gate_values.T, wg[0], wu[0], wd[0],
        gf[0].T, gs[0], uf[0].T, us[0], df[0].T, ds[0],
    )
    tg, gg, ggi, ggo, gui, guo, gdi, gdo = pl.pallas_call(
        combine_kernel,
        out_shape=(
            shape((TD, D), bf16),
            shape((2, TD), f32),
            shape((16, D), f32),
            shape((16, F), f32),
            shape((16, D), f32),
            shape((16, F), f32),
            shape((16, F), f32),
            shape((16, D), f32),
        ),
        in_specs=[vmem] * 5,
        out_specs=[vmem] * 8,
        scratch_shapes=[pltpu.VMEM((NE, D), bf16)],
        compiler_params=pltpu.CompilerParams(vmem_limit_bytes=32 * 2**20),
    )(blocks, sel, permT, sums, expert_ids.T)
    return tg, gg.T, ggi.T[None], ggo[None], gui.T[None], guo[None], gdi.T[None], gdo[None]


def solution(mesh):
    row = P(("dp", "expert"), None)
    frozen = P("expert", "dp", None)
    one = P("expert", None, None)
    return jax.shard_map(
        per_device,
        mesh=mesh,
        in_specs=(row,) * 4 + (frozen,) * 3 + (one,) * 6,
        out_specs=(row,) * 2 + (one,) * 6,
        check_vma=False,
    )
```

time: 213 us -> 209 us (0.981)
  local copies, waits for them, and re-layouts: 6.7 us -> 4.37 us
    unnamed x22 -> x10, local copies, waits for them, and re-layouts: 6.7 us -> 4.37 us
    pallas_call x1 -> x2, Pallas kernels: 205 us -> 204 us  [the longest x1 201 us: per_device(): pl.pallas_call(kernel, out_shape=(shape((512, BW), bf16), shape((512, 2 *...]
where the time goes in v4:
time: 209 us
  Pallas kernels  204 us (98%)
  local copies, waits for them, and re-layouts  4.37 us (2%)
    pallas_call x1, Pallas kernels, per_device(): pl.pallas_call(kernel, out_shape=(shape((512, BW), bf16), shape((512, 2 *...  201 us
    unnamed x10, local copies, waits for them, and re-layouts  4.37 us

profile of v4, /device:TPU:1, one launch (start us, length us, event | category | flops | bytes accessed | tf_op | source)
XLA Modules:
  0.0 208.6 jit_solution(14360775666482944495)
XLA Ops:
  0.6 0.0 copy-start.4
  0.6 200.6 %shard_map.188 = (bf16[512,1536]{1,0:T(8,128)(2,1)}, bf16[512,256]{1,0:T(8,128)(2,1)}, bf16[512,512]{1,0:T(8,128)(2,1)}, bf16[16,16,640]{2,1,0:T(8,128)(2,1)}) custom-call(bf16[128,2560]{1,0:T(8,128)(2,1)} %tok.1, bf16[128,2560]{1,0:T(8,128)(2,1)} %grd.1, s32[2,128]{1,0:T(2,128)} %bitcast.30, f32[2,128]{1,0:T(2,128)} %bitcast.47, bf16[160,768]{1,0:T(8,128)(2,1)} %bitcast.32, ...), custom_call_target="tpu_custom_call" | custom-call | flops 8000000000 | bytes 20000000 | tf_op jit(solution)/shard_map/pallas_call | solution.py:613
  201.2 0.0 copy-done.4
  201.3 0.0 copy-start
  201.3 1.4 copy-done
  202.7 0.0 copy-start.1
  202.7 1.0 copy-done.1
  203.7 0.0 copy-start.2
  203.7 1.0 copy-done.2
  204.7 0.0 copy-start.3
  204.7 0.9 copy-done.3
  205.6 3.0 %shard_map.189 = (bf16[128,2560]{1,0:T(8,128)(2,1)}, f32[2,128]{1,0:T(2,128)}, f32[16,2560]{1,0:T(8,128)}, f32[16,768]{1,0:T(8,128)}, f32[16,2560]{1,0:T(8,128)}...) custom-call(bf16[512,1536]{1,0:T(8,128)(2,1)S(1)} %copy-done, bf16[512,256]{1,0:T(8,128)(2,1)S(1)} %copy-done.3, ...), custom_call_target="tpu_custom_call" | custom-call | tf_op jit(solution)/shard_map/pallas_call | solution.py:685
Async XLA Ops:
  0.6 200.6 %copy-start.4 = (s32[128,2]{0,1:T(2,128)S(1)}, s32[128,2]{0,1:T(2,128)}, u32[]{:S(2)}) copy-start(s32[128,2]{0,1:T(2,128)} %param.15) | copy-start | bytes 3076
  201.3 1.4 copy-start
  202.7 1.0 copy-start.1
  203.7 1.0 copy-start.2
  204.7 0.9 copy-start.3

commit v5 on v4

--- a/solution.py
+++ b/solution.py
@@ -140,7 +140,7 @@
         loop(NE - 1, body)
         recv[buf, block(my_slot), :] = send[buf, block(mine), :]
 
-    CUT = 512
+    CUT = 768
 
     def back_copy(part, src, dst, d, e):
         c = pl.ds(0, CUT) if part == 0 else pl.ds(CUT, BW - CUT)

time: 209 us -> 209 us (level)
  no operation moved by 1% of the time
where the time goes in v5:
time: 209 us
  Pallas kernels  204 us (98%)
  local copies, waits for them, and re-layouts  4.37 us (2%)
    pallas_call x1, Pallas kernels, per_device(): pl.pallas_call(kernel, out_shape=(shape((512, BW), bf16), shape((512, 2 *...  201 us
    unnamed x10, local copies, waits for them, and re-layouts  4.37 us

profile of v5, /device:TPU:1, one launch (start us, length us, event | category | flops | bytes accessed | tf_op | source)
XLA Modules:
  0.0 209.1 jit_solution(3866216193343187674)
XLA Ops:
  0.6 0.0 copy-start.4
  0.6 201.0 %shard_map.188 = (bf16[512,1536]{1,0:T(8,128)(2,1)}, bf16[512,256]{1,0:T(8,128)(2,1)}, bf16[512,512]{1,0:T(8,128)(2,1)}, bf16[16,16,640]{2,1,0:T(8,128)(2,1)}) custom-call(bf16[128,2560]{1,0:T(8,128)(2,1)} %tok.1, bf16[128,2560]{1,0:T(8,128)(2,1)} %grd.1, s32[2,128]{1,0:T(2,128)} %bitcast.30, f32[2,128]{1,0:T(2,128)} %bitcast.47, bf16[160,768]{1,0:T(8,128)(2,1)} %bitcast.32, ...), custom_call_target="tpu_custom_call" | custom-call | flops 8000000000 | bytes 20000000 | tf_op jit(solution)/shard_map/pallas_call | solution.py:613
  201.7 0.0 copy-done.4
  201.7 0.0 copy-start
  201.7 1.4 copy-done
  203.1 0.0 copy-start.1
  203.1 1.0 copy-done.1
  204.1 0.0 copy-start.2
  204.1 1.0 copy-done.2
  205.1 0.0 copy-start.3
  205.1 0.9 copy-done.3
  206.1 3.0 %shard_map.189 = (bf16[128,2560]{1,0:T(8,128)(2,1)}, f32[2,128]{1,0:T(2,128)}, f32[16,2560]{1,0:T(8,128)}, f32[16,768]{1,0:T(8,128)}, f32[16,2560]{1,0:T(8,128)}...) custom-call(bf16[512,1536]{1,0:T(8,128)(2,1)S(1)} %copy-done, bf16[512,256]{1,0:T(8,128)(2,1)S(1)} %copy-done.3, ...), custom_call_target="tpu_custom_call" | custom-call | tf_op jit(solution)/shard_map/pallas_call | solution.py:685
Async XLA Ops:
  0.6 201.0 %copy-start.4 = (s32[128,2]{0,1:T(2,128)S(1)}, s32[128,2]{0,1:T(2,128)}, u32[]{:S(2)}) copy-start(s32[128,2]{0,1:T(2,128)} %param.15) | copy-start | bytes 3076
  201.7 1.4 copy-start
  203.1 1.0 copy-start.1
  204.1 1.0 copy-start.2
  205.1 0.9 copy-start.3
